TPU v7x, 256 devices: a whole 4x4x8 slice. The times are simulated.
256 devices in a mesh: slab: 16 (over z, y_lo), blk: 16 (over y_hi, x, core).
Axes of the slice: x: 4, y: 4 (y_hi: 2, y_lo: 2; y = y_hi * 2 + y_lo), z: 8, core: 2. Of those that a mesh axis runs over, the one named last changes fastest.
Arguments:
- row_emb: float32 [196608, 256], P(('slab', 'blk')), may hold values from -1.5 to 1.5
- col_emb: float32 [196608, 256], P(('slab', 'blk')), may hold values from -1.5 to 1.5
- row_acc: float32 [196608], P(('slab', 'blk')), may hold values from 100000 to 1000000
- col_acc: float32 [196608], P(('slab', 'blk')), may hold values from 100000 to 1000000
- counts: int32 [196608, 4, 768], P(('slab', 'blk')), may hold values from 0 to 1764, as said below
- marginal: int32 [196608], P('slab'), may hold values from 1000 to 90000, as said below
Outputs:
- new_row_emb: float32 [196608, 256], P(('slab', 'blk'))
- new_col_emb: float32 [196608, 256], P(('slab', 'blk'))
- new_row_acc: float32 [196608], P(('slab', 'blk'))
- new_col_acc: float32 [196608], P(('slab', 'blk'))
Inputs may be any that keep to these rules, and one draw needn't show every extreme that they name: `counts`: zero or a positive count; some entry equals 1764. Some item has marginal 1000 and some 90000.
All inputs are finite; a program needn't handle non-finite values.
Results may differ from a plain program's by a relative error of at most 0.0075.
Values may be sent and summed in bfloat16 or wider, within the bound.
No kernel may reach another device: no remote copies, remote signals or barrier semaphores. Data moves between devices by JAX's collectives and lax.ppermute only.
A program may use at most 128 MiB of HBM per device.

v0:
```python
import functools

import jax
import jax.numpy as jnp
from jax import lax
from jax.experimental import pallas as pl
from jax.experimental.pallas import tpu as pltpu
from jax.sharding import PartitionSpec as P

learn_rate = 0.5
f32, bf16 = jnp.float32, jnp.bfloat16
VMEM = pl.BlockSpec(memory_space=pltpu.VMEM)
SMEM = pl.BlockSpec(memory_space=pltpu.SMEM)
ANY = pl.BlockSpec(memory_space=pl.ANY)
LARGE = pl.CostEstimate(flops=1 << 37, bytes_accessed=1 << 30, transcendentals=0)
GRANT = 20 << 20
SMALL = pl.CostEstimate(flops=1 << 20, bytes_accessed=1 << 10, transcendentals=0)
RELAY = True
FAR = (768,)


def halves_kernel(row_emb, col_emb, *outs):
    start = 0
    for out in outs:
        span = out.shape[0] // 2
        out[:span, :] = row_emb[pl.ds(start, span), :].astype(bf16)
        out[span:, :] = col_emb[pl.ds(start, span), :].astype(bf16)
        start += span


def rounded(row_emb, col_emb, spans):
    width = row_emb.shape[1]
    return pl.pallas_call(
        halves_kernel,
        in_specs=[VMEM] * 2,
        out_specs=[VMEM] * len(spans),
        out_shape=[jax.ShapeDtypeStruct((2 * span, width), bf16) for span in spans],
        compiler_params=pltpu.CompilerParams(vmem_limit_bytes=8 << 20),
        cost_estimate=SMALL,
        name="rounded",
    )(row_emb, col_emb)


def turned_kernel(row_emb, col_emb, own_half, own_t):
    block, width = row_emb.shape
    for side, emb in enumerate((row_emb, col_emb)):
        values = emb[...].astype(bf16)
        own_half[pl.ds(side * block, block), :] = values * bf16(0.5)
        own_t[pl.ds(side * width, width), :] = values.T


def turned(row_emb, col_emb):
    block, width = row_emb.shape
    return pl.pallas_call(
        turned_kernel,
        in_specs=[VMEM] * 2,
        out_specs=[VMEM] * 2,
        out_shape=[
            jax.ShapeDtypeStruct((2 * block, width), bf16),
            jax.ShapeDtypeStruct((2 * width, block), bf16),
        ],
        compiler_params=pltpu.CompilerParams(vmem_limit_bytes=8 << 20),
        cost_estimate=SMALL,
        name="turned",
    )(row_emb, col_emb)


def lay_kernel(k_ref, counts, *refs):
    outs, held, sems_in, sems_out = refs[:-3], refs[-3], refs[-2], refs[-1]
    copies = [
        pltpu.make_async_copy(counts.at[:, k_ref[i], :], held.at[i], sems_in.at[i])
        for i in range(len(outs))
    ]
    for copy in copies:
        copy.start()
    leaving = []
    for i, out in enumerate(outs):
        copies[i].wait()
        leaving.append(pltpu.make_async_copy(held.at[i], out, sems_out.at[i]))
        leaving[-1].start()
    for copy in leaving:
        copy.wait()


def lay(offsets, counts):
    block, _, width = counts.shape
    steps = len(offsets)
    return pl.pallas_call(
        lay_kernel,
        in_specs=[SMEM, ANY],
        out_specs=[ANY] * steps,
        out_shape=[jax.ShapeDtypeStruct((block, width), jnp.int32)] * steps,
        scratch_shapes=[
            pltpu.VMEM((steps, block, width), jnp.int32),
            pltpu.SemaphoreType.DMA((steps,)),
            pltpu.SemaphoreType.DMA((steps,)),
        ],
        compiler_params=pltpu.CompilerParams(vmem_limit_bytes=56 << 20),
        cost_estimate=SMALL,
        name="lay",
    )(jnp.stack(offsets), counts)


def tile_kernel(
    even_ref, laid, total, more_total, lm_rows, lm_cols, own_half, own_t, *refs,
    start, span, rows, cols, kind,
):
    block = own_half.shape[0] // 2
    width = own_half.shape[1]
    parts = refs[: {"whole": 1, "halves": 2, "either": 3}[kind]]
    acc_in, acc, back_row, back_col, tiles, sems = refs[len(parts) :]
    even = even_ref[0] == 1

    def partner(side, j):
        if kind == "whole":
            return parts[0][pl.ds(side * block + start + j * cols, cols), :]
        if kind == "halves":
            return parts[side][pl.ds(start + j * cols, cols), :]
        return jnp.where(
            even,
            parts[side][pl.ds(start + j * cols, cols), :],
            parts[2][pl.ds(side * block + start + j * cols, cols), :],
        )

    copies = [
        pltpu.make_async_copy(
            laid.at[:, pl.ds(start + j * cols, cols)],
            tiles.at[:, pl.ds(j * cols, cols)],
            sems.at[j],
        )
        for j in range(span // cols)
    ]
    copies[0].start()
    half_log = 0.5 * jnp.log(jnp.sum(total[...] + more_total[...], keepdims=True))
    dims = (((1,), (1,)), ((), ()))
    for j in range(span // cols):
        js = pl.ds(j * cols, cols)
        where = pl.ds(start + j * cols, cols)
        copies[j].wait()
        if j + 1 < len(copies):
            copies[j + 1].start()
        row_part, col_part = partner(0, j), partner(1, j)
        backs = [None, None]
        for i in range(block // rows):
            mine = pl.ds(i * rows, rows)
            seen_counts = tiles[mine, js]
            positive = seen_counts > 0
            safe = jnp.maximum(seen_counts.astype(f32), 1.0)
            goal = 0.5 * jnp.log(safe) + (half_log - 0.5 * lm_rows[mine, :]) - 0.5 * lm_cols[:, where]
            sure = 0.2 + (0.5 * safe) * lax.rsqrt(safe)
            for side, seen in enumerate((col_part, row_part)):
                at = pl.ds(side * block + i * rows, rows)
                logits = lax.dot_general(own_half[at, :], seen, dims, preferred_element_type=f32)
                differ = logits - goal
                grad = jnp.where(positive, sure * differ, 0.5 * jnp.tanh(differ) + 0.5).astype(bf16)
                source = acc_in if j == 0 else acc
                acc[at, :] = source[at, :] + jnp.dot(grad, seen, preferred_element_type=f32)
                more = jnp.dot(
                    own_t[pl.ds(side * width, width), mine], grad, preferred_element_type=f32
                )
                backs[side] = more if backs[side] is None else backs[side] + more
        back_col[:, js] = backs[0].astype(bf16)
        back_row[:, js] = backs[1].astype(bf16)


def tile(even, laid, totals, lm_rows, lm_cols, own_half, own_t, parts, acc, start, span, rows=768, cols=256):
    block, width = own_half.shape[0] // 2, own_half.shape[1]
    cols = min(cols, span)
    kind = ("whole", "halves", "either")[len(parts) - 1]
    return pl.pallas_call(
        functools.partial(tile_kernel, start=start, span=span, rows=rows, cols=cols, kind=kind),
        in_specs=[SMEM, ANY] + [VMEM] * (7 + len(parts)),
        out_specs=[VMEM] * 3,
        out_shape=[jax.ShapeDtypeStruct((2 * block, width), f32)]
        + [jax.ShapeDtypeStruct((width, span), bf16)] * 2,
        scratch_shapes=[
            pltpu.VMEM((block, span), jnp.int32),
            pltpu.SemaphoreType.DMA((span // cols,)),
        ],
        input_output_aliases={8 + len(parts): 0},
        compiler_params=pltpu.CompilerParams(vmem_limit_bytes=GRANT),
        cost_estimate=SMALL,
        name="tile",
    )(even, laid, *totals, lm_rows, lm_cols, own_half, own_t, *parts, acc)


def join_kernel(even_ref, row_here, col_here, row_there, col_there, out):
    width = row_here.shape[0]

    @pl.when(even_ref[0] == 1)
    def _():
        out[:width, :] = row_here[...] + row_there[...]
        out[width:, :] = col_here[...] + col_there[...]

    @pl.when(even_ref[0] != 1)
    def _():
        out[:width, :] = row_there[...]
        out[width:, :] = col_there[...]


def join(even, here, there):
    width, span = here[0].shape
    return pl.pallas_call(
        join_kernel,
        in_specs=[SMEM] + [VMEM] * 4,
        out_specs=VMEM,
        out_shape=jax.ShapeDtypeStruct((2 * width, span), bf16),
        compiler_params=pltpu.CompilerParams(vmem_limit_bytes=8 << 20),
        cost_estimate=SMALL,
        name="join",
    )(even, *here, *there)


def gather_kernel(even_ref, acc, *refs, counts):
    near, chip, out = refs[: counts[0]], refs[counts[0] : -1], refs[-1]
    width = out.shape[0] // 2
    block = out.shape[1]
    even = even_ref[0] == 1
    for half in range(2):
        cut = pl.ds(half * width, width)
        out[cut, :] = acc[pl.ds(half * block, block), :].T
        for pieces, ours in ((near, None), (chip, even)):
            start = 0
            for piece in pieces:
                items = pl.ds(start, piece.shape[1])
                start += piece.shape[1]
                more = piece[cut, :].astype(f32)
                out[cut, items] += more if ours is None else jnp.where(ours, more, 0.0)


def gather_up(even, acc, near, chip):
    width, block = acc.shape[1], acc.shape[0] // 2
    return pl.pallas_call(
        functools.partial(gather_kernel, counts=(len(near), len(chip))),
        in_specs=[SMEM] + [VMEM] * (1 + len(near) + len(chip)),
        out_specs=VMEM,
        out_shape=jax.ShapeDtypeStruct((2 * width, block), f32),
        compiler_params=pltpu.CompilerParams(vmem_limit_bytes=16 << 20),
        cost_estimate=LARGE,
        name="gather_up",
    )(even, acc, *near, *chip)


def update_kernel(even_ref, row_emb, col_emb, row_acc, col_acc, grads, *refs):
    pieces = (len(refs) - 4) // 3
    far, chips = refs[:pieces], refs[pieces:-4]
    even = even_ref[0] == 1
    new_row, new_col, new_racc, new_cacc = refs[-4:]
    block, width = row_emb.shape
    sides = ((row_emb, row_acc, new_row, new_racc), (col_emb, col_acc, new_col, new_cacc))
    for half, (emb, accum, new_emb, new_accum) in enumerate(sides):
        cut = pl.ds(half * width, width)
        start = 0
        for piece, beside in zip(far, chips[half::2]):
            items = pl.ds(start, piece.shape[1])
            start += piece.shape[1]
            grad = grads[cut, items] + piece[cut, :].astype(f32)
            grad += jnp.where(even, beside[...].astype(f32), 0.0)
            total = accum[:, items] + jnp.sum(grad * grad, axis=0, keepdims=True) * (1.0 / width)
            for lane in range(items.start, items.start + items.size, 128):
                new_accum[lane // 128, :] = total[0, lane - items.start : lane - items.start + 128]
            step = grad * (learn_rate * lax.rsqrt(total))
            new_emb[items, :] = emb[items, :] - step.T


def update(even, row_emb, col_emb, row_acc, col_acc, grads, far, chip):
    block, width = row_emb.shape
    return pl.pallas_call(
        update_kernel,
        in_specs=[SMEM] + [VMEM] * (5 + 3 * len(far)),
        out_specs=[VMEM] * 4,
        out_shape=[jax.ShapeDtypeStruct((block, width), f32)] * 2
        + [jax.ShapeDtypeStruct((block // 128, 128), f32)] * 2,
        compiler_params=pltpu.CompilerParams(vmem_limit_bytes=16 << 20),
        cost_estimate=SMALL,
        name="update",
    )(even, row_emb, col_emb, row_acc, col_acc, grads, *far, *chip)


def per_device(row_emb, col_emb, row_acc, col_acc, counts, marginal):
    cycle = lax.axis_size("blk")
    me = lax.axis_index("blk")
    odd = me % 2 == 1
    even = jnp.where(odd, 0, 1).astype(jnp.int32).reshape(1)
    block, width = row_emb.shape

    def moved(array, distance_even, distance_odd=None):
        distance_odd = distance_even if distance_odd is None else distance_odd
        route = [(i, (i + (distance_odd if i % 2 else distance_even)) % cycle) for i in range(cycle)]
        return lax.ppermute(array, "blk", route)

    def swapped(array):
        return moved(array, 1, -1)

    def starts_of(spans):
        return [sum(spans[:i]) for i in range(len(spans))]

    shift_near = jnp.where(odd, 3, 1)
    shift_far = jnp.where(odd, 1, 3)

    marg_f = marginal.astype(f32)
    total = jnp.sum(marg_f.reshape(-1, 8, 128), axis=0)
    slabs = lax.axis_size("slab")

    def from_reach(total, reach):
        return lax.ppermute(total, "slab", [(i, i ^ reach) for i in range(slabs)])

    there = from_reach(total, 1)
    (piece,) = rounded(row_emb, col_emb, (block,))
    near_in = moved(piece, 2)
    shifts = [jnp.int32(2), shift_near, jnp.int32(4), shift_far]
    offsets = [shift - 1 for shift in shifts]
    *first, piece = lax.optimization_barrier((*offsets[:2], piece))
    laid = lay(first, counts)
    *laid, there = lax.optimization_barrier((*laid, there))
    total = total + there
    there = from_reach(total, 2)
    *second, total = lax.optimization_barrier((*offsets[2:], total))
    later = lay(second, counts)
    *later, there = lax.optimization_barrier((*later, there))
    laid = [*laid, *later]
    total = total + there
    there = from_reach(total, 4)
    total = total + there
    there = from_reach(total, 8)
    near_in, total = lax.optimization_barrier((near_in, total))
    far_in = moved(near_in if RELAY else piece, 2 if RELAY else 4)
    row_again, col_again, total = lax.optimization_barrier((row_emb, col_emb, total))
    own_half, own_t = turned(row_again, col_again)
    totals = (total, there)
    log_marg = jnp.log(marg_f).reshape(cycle, 1, block)

    def log_marg_of(place):
        return lax.dynamic_index_in_dim(log_marg, place % cycle, keepdims=False)

    lm_rows = log_marg_of(me).reshape(block, 1)
    acc = jnp.zeros((2 * block, width), f32)
    def tiles(slot, parts, acc, start, span):
        acc, *backs = tile(
            even, laid[slot], totals, lm_rows, log_marg_of(me - shifts[slot]), own_half, own_t, parts,
            acc, start, span,
        )
        return acc, backs

    def both(function, arrays):
        return [function(array) for array in arrays]

    other = swapped(near_in)
    acc, back_two = tiles(0, [near_in], acc, 0, block)
    from_other = both(swapped, back_two)
    acc, back_near = tiles(1, [other], acc, 0, block)
    joined = join(jnp.ones_like(even), back_near, from_other)
    near_out = [moved(joined, -1, -3)]
    acc, joined = lax.optimization_barrier((acc, joined))
    chip_out, far_out = [], []
    to_even = [(i, i - 1) for i in range(1, cycle, 2)]
    to_odd = [(i, i + 1) for i in range(0, cycle, 2)]
    beside = lax.ppermute(piece, "blk", to_odd)
    other = [lax.ppermute(far_in[i * block : (i + 1) * block], "blk", to_even) for i in range(2)]
    for start, span in zip(starts_of(FAR), FAR):
        acc, back_four = tiles(2, [far_in], acc, start, span)
        from_other = both(swapped, back_four)
        acc, back_far = tiles(3, [*other, beside], acc, start, span)
        joined = join(even, back_far, from_other)
        far_out.append(moved(joined, -3, -5))
        acc, joined = lax.optimization_barrier((acc, joined))
        chip_out += both(swapped, back_far)
    grads = gather_up(even, acc, near_out, [])
    new_rows, new_cols, new_racc, new_cacc = update(
        even, row_emb, col_emb, row_acc.reshape(1, block), col_acc.reshape(1, block), grads, far_out, chip_out
    )
    return (new_rows, new_cols, new_racc.reshape(block), new_cacc.reshape(block))


def solution(mesh):
    in_specs = (
        P(("slab", "blk"), None),
        P(("slab", "blk"), None),
        P(("slab", "blk")),
        P(("slab", "blk")),
        P(("slab", "blk"), None, None),
        P("slab"),
    )
    out_specs = (
        P(("slab", "blk"), None),
        P(("slab", "blk"), None),
        P(("slab", "blk")),
        P(("slab", "blk")),
    )
    return jax.shard_map(
        per_device, mesh=mesh, in_specs=in_specs, out_specs=out_specs, check_vma=False
    )
```

profile of v0, /device:TPU:7, one launch (start us, length us, event | category | flops | bytes accessed | tf_op | source)
XLA Modules:
  0.0 93.8 jit_solution(12671259569215613840)
XLA Ops:
  0.6 0.0 copy-start
  0.6 1.1 %copy-done = f32[768,256]{1,0:T(8,128)S(1)} copy-done((f32[768,256]{1,0:T(8,128)S(1)}, f32[768,256]{1,0:T(8,128)}, u32[]{:S(2)}) %copy-start) | copy-done | bytes 786456
  1.8 1.1 %copy-done.2 = f32[768,256]{1,0:T(8,128)S(1)} copy-done((f32[768,256]{1,0:T(8,128)S(1)}, f32[768,256]{1,0:T(8,128)}, u32[]{:S(2)}) %copy-start.2) | copy-done | bytes 786456
  2.9 0.1 rounded.1
  3.0 2.9 %collective-permute-start.2 = (bf16[1536,256]{1,0:T(8,128)(2,1)S(1)}, bf16[1536,256]{1,0:T(8,128)(2,1)}, u32[]{:S(2)}, u32[]{:S(2)}) collective-permute-start(bf16[1536,256]{1,0:T(8,128)(2,1)S(1)} %rounded.1), channel_id=1, source_target_pairs={{0,2},{1,3},{2,4},{3,5},{4,6},{5,7},{6,8},{7,9},{8,10},{9,11},{10,... | collective-permute-start | bytes 2359304 | tf_op jit(solution)/shard_map/ppermute | solution.py:290
  5.9 0.5 collective-permute-start
  6.4 0.6 pad_add_fusion.k_ref
  7.0 4.6 %lay.2 = (s32[768,768]{1,0:T(8,128)}, s32[768,768]{1,0:T(8,128)}) custom-call(s32[2]{0:T(128)} %pad_add_fusion.k_ref, s32[768,4,768]{2,1,0:T(4,128)} %counts.3), custom_call_target="tpu_custom_call" | custom-call | flops 1048576 | bytes 1024 | tf_op jit(solution)/shard_map/lay/pallas_call | solution.py:88
  11.6 0.0 collective-permute-done
  11.6 1.7 %collective-permute-start.1 = (f32[8,128]{1,0:T(8,128)S(1)}, f32[8,128]{1,0:T(8,128)S(1)}, u32[]{:S(2)}, u32[]{:S(2)}) collective-permute-start(f32[8,128]{1,0:T(8,128)S(1)} %add.49), channel_id=1, source_target_pairs={{0,32},{16,48},{32,0},{48,16},{64,96},{80,112},{96,64},{112,80},{1... | collective-permute-start | bytes 12296 | tf_op jit(solution)/shard_map/ppermute | solution.py:306
  13.3 0.6 pad_add_fusion.1.k_ref
  13.9 4.7 %lay.3 = (s32[768,768]{1,0:T(8,128)}, s32[768,768]{1,0:T(8,128)}) custom-call(s32[2]{0:T(128)} %pad_add_fusion.1.k_ref, s32[768,4,768]{2,1,0:T(4,128)} %counts.3), custom_call_target="tpu_custom_call" | custom-call | flops 1048576 | bytes 1024 | tf_op jit(solution)/shard_map/lay/pallas_call | solution.py:88
  18.6 0.0 collective-permute-done.1
  18.6 3.1 %collective-permute-start.3 = (f32[8,128]{1,0:T(8,128)S(1)}, f32[8,128]{1,0:T(8,128)S(1)}, u32[]{:S(2)}, u32[]{:S(2)}) collective-permute-start(f32[8,128]{1,0:T(8,128)S(1)} %add.50), channel_id=1, source_target_pairs={{0,64},{16,80},{32,96},{48,112},{64,0},{80,16},{96,32},{112,48},{1... | collective-permute-start | bytes 12296 | tf_op jit(solution)/shard_map/ppermute | solution.py:306
  21.7 1.3 %collective-permute-start.8 = (bf16[1536,256]{1,0:T(8,128)(2,1)S(1)}, bf16[1536,256]{1,0:T(8,128)(2,1)}, u32[]{:S(2)}, u32[]{:S(2)}) collective-permute-start(bf16[1536,256]{1,0:T(8,128)(2,1)S(1)} %rounded.1), channel_id=1, source_target_pairs={{0,1},{2,3},{4,5},{6,7},{8,9},{10,11},{12,13},{14,15},{16,17},{18,... | collective-permute-start | bytes 2359304 | tf_op jit(solution)/shard_map/ppermute | solution.py:358
  23.0 0.0 collective-permute-done.3
  23.0 0.0 collective-permute-done.2.refs_0_
  23.0 2.8 %collective-permute-start.9 = (bf16[1536,256]{1,0:T(8,128)(2,1)}, bf16[1536,256]{1,0:T(8,128)(2,1)}, u32[]{:S(2)}, u32[]{:S(2)}) collective-permute-start(bf16[1536,256]{1,0:T(8,128)(2,1)} %collective-permute-done.2.refs_0_), channel_id=1, source_target_pairs={{0,1},{1,0},{2,3},{3,2},{4,5},{5,4},{6,7},{7,6},{8,9},{9,8},{10,11... | collective-permute-start | bytes 2359304 | tf_op jit(solution)/shard_map/ppermute | solution.py:290
  25.8 3.8 %collective-permute-start.5 = (bf16[1536,256]{1,0:T(8,128)(2,1)}, bf16[1536,256]{1,0:T(8,128)(2,1)S(1)}, u32[]{:S(2)}, u32[]{:S(2)}) collective-permute-start(bf16[1536,256]{1,0:T(8,128)(2,1)} %collective-permute-done.2.refs_0_), channel_id=1, source_target_pairs={{0,2},{1,3},{2,4},{3,5},{4,6},{5,7},{6,8},{7,9},{8,10},{9,11},{10,... | collective-permute-start | bytes 2359304 | tf_op jit(solution)/shard_map/ppermute | solution.py:290
  29.7 7.0 %collective-permute-start.4 = (f32[8,128]{1,0:T(8,128)S(1)}, f32[8,128]{1,0:T(8,128)S(1)}, u32[]{:S(2)}, u32[]{:S(2)}) collective-permute-start(f32[8,128]{1,0:T(8,128)S(1)} %add.51.total), channel_id=1, source_target_pairs={{0,128},{16,144},{32,160},{48,176},{64,192},{80,208},{96,224},{112... | collective-permute-start | bytes 12296 | tf_op jit(solution)/shard_map/ppermute | solution.py:306
  36.7 0.6 dynamic-slice_bitcast_fusion
  37.3 0.9 copy.21.lm_rows
  38.1 0.0 copy-done.1
  38.1 0.0 copy-done.3
  38.2 0.0 copy-start.6
  38.2 0.0 copy-start.9
  38.2 0.3 turned.1
  38.4 0.0 collective-permute-done.4.more_total
  38.5 0.1 broadcast_in_dim.3.refs_1_
  38.6 1.3 %copy-done.6 = s32[768,768]{1,0:T(8,128)S(1)} copy-done((s32[768,768]{1,0:T(8,128)S(1)}, s32[768,768]{1,0:T(8,128)}, u32[]{:S(2)}) %copy-start.6) | copy-done | bytes 2359320
  39.8 5.3 %tile.4 = (f32[1536,256]{1,0:T(8,128)S(1)}, bf16[256,768]{1,0:T(8,128)(2,1)S(1)}, bf16[256,768]{1,0:T(8,128)(2,1)S(1)}) custom-call(s32[1]{0:T(128)} %bitcast.even_ref, s32[768,768]{1,0:T(8,128)S(1)} %copy-done.6, f32[8,128]{1,0:T(8,128)S(1)} %add.51.total, f32[8,128]{1,0:T(8,128)S(1)} %collective-permute-done.4.more_total, ...), custom_call_target="tpu_custom_call", output_to_operand_aliasing={{0}: (9, {})} | custom-call | flops 1048576 | bytes 1024 | tf_op jit(solution)/shard_map/tile/pallas_call | solution.py:170
  45.1 0.7 collective-permute-start.10
  45.8 0.3 collective-permute-start.11
  46.0 0.0 collective-permute-done.9.refs_0_
  46.1 5.1 %tile.5 = (f32[1536,256]{1,0:T(8,128)S(1)}, bf16[256,768]{1,0:T(8,128)(2,1)S(1)}, bf16[256,768]{1,0:T(8,128)(2,1)S(1)}) custom-call(s32[1]{0:T(128)} %bitcast.even_ref, s32[768,768]{1,0:T(8,128)S(1)} %copy-done.5, f32[8,128]{1,0:T(8,128)S(1)} %add.51.total, f32[8,128]{1,0:T(8,128)S(1)} %collective-permute-done.4.more_total, ...), custom_call_target="tpu_custom_call", output_to_operand_aliasing={{0}: (9, {})} | custom-call | flops 1048576 | bytes 1024 | tf_op jit(solution)/shard_map/tile/pallas_call | solution.py:170
  51.2 0.0 collective-permute-done.10.row_there
  51.2 0.0 collective-permute-done.11.col_there
  51.2 0.1 join.2
  51.3 0.1 collective-permute-start.14
  51.4 0.0 collective-permute-done.5.refs_0_
  51.4 0.1 fusion
  51.5 2.3 %collective-permute-start.6 = (bf16[768,256]{1,0:T(8,128)(2,1)S(1)}, bf16[768,256]{1,0:T(8,128)(2,1)S(1)}, u32[]{:S(2)}, u32[]{:S(2)}) collective-permute-start(bf16[768,256]{1,0:T(8,128)(2,1)S(1)} %get-tuple-element.87), channel_id=1, source_target_pairs={{1,0},{3,2},{5,4},{7,6},{9,8},{11,10},{13,12},{15,14},{17,16},{19,... | collective-permute-start | bytes 1179656 | tf_op jit(solution)/shard_map/ppermute | solution.py:359
  53.8 1.3 %collective-permute-start.7 = (bf16[768,256]{1,0:T(8,128)(2,1)S(1)}, bf16[768,256]{1,0:T(8,128)(2,1)S(1)}, u32[]{:S(2)}, u32[]{:S(2)}) collective-permute-start(bf16[768,256]{1,0:T(8,128)(2,1)S(1)} %get-tuple-element.86), channel_id=1, source_target_pairs={{1,0},{3,2},{5,4},{7,6},{9,8},{11,10},{13,12},{15,14},{17,16},{19,... | collective-permute-start | bytes 1179656 | tf_op jit(solution)/shard_map/ppermute | solution.py:359
  55.1 0.0 copy-start.11
  55.1 0.0 copy-start.12
  55.2 4.0 %tile.6 = (f32[1536,256]{1,0:T(8,128)S(1)}, bf16[256,768]{1,0:T(8,128)(2,1)S(1)}, bf16[256,768]{1,0:T(8,128)(2,1)S(1)}) custom-call(s32[1]{0:T(128)} %bitcast.even_ref, s32[768,768]{1,0:T(8,128)S(1)} %copy-done.4, f32[8,128]{1,0:T(8,128)S(1)} %add.51.total, f32[8,128]{1,0:T(8,128)S(1)} %collective-permute-done.4.more_total, ...), custom_call_target="tpu_custom_call", output_to_operand_aliasing={{0}: (9, {})} | custom-call | flops 1048576 | bytes 1024 | tf_op jit(solution)/shard_map/tile/pallas_call | solution.py:170
  59.2 0.1 collective-permute-start.12
  59.3 0.0 collective-permute-done.8.refs_2_
  59.3 0.5 collective-permute-start.13
  59.8 0.0 collective-permute-done.6.refs_0_
  59.8 0.0 collective-permute-done.7.refs_1_
  59.8 5.2 %tile.7 = (f32[1536,256]{1,0:T(8,128)S(1)}, bf16[256,768]{1,0:T(8,128)(2,1)S(1)}, bf16[256,768]{1,0:T(8,128)(2,1)S(1)}) custom-call(s32[1]{0:T(128)} %bitcast.even_ref, s32[768,768]{1,0:T(8,128)S(1)} %copy-done.7, f32[8,128]{1,0:T(8,128)S(1)} %add.51.total, f32[8,128]{1,0:T(8,128)S(1)} %collective-permute-done.4.more_total, ...), custom_call_target="tpu_custom_call", output_to_operand_aliasing={{0}: (11, {})} | custom-call | flops 1048576 | bytes 1024 | tf_op jit(solution)/shard_map/tile/pallas_call | solution.py:170
  65.0 0.4 collective-permute-start.16
  65.4 0.2 collective-permute-start.17
  65.6 0.0 collective-permute-done.12.row_there
  65.6 0.0 collective-permute-done.13.col_there
  65.6 0.1 join.3
  65.7 0.1 collective-permute-start.15
  65.8 25.5 %collective-permute-done.14.refs_0_ = bf16[512,768]{1,0:T(8,128)(2,1)S(1)} collective-permute-done((bf16[512,768]{1,0:T(8,128)(2,1)S(1)}, bf16[512,768]{1,0:T(8,128)(2,1)S(1)}, u32[]{:S(2)}, u32[]{:S(2)}) %collective-permute-start.14) | collective-permute-done | bytes 786464 | tf_op jit(solution)/shard_map/ppermute | solution.py:290
  91.3 0.5 gather_up.1.grads
  91.7 0.0 collective-permute-done.16.refs_1_
  91.7 0.0 collective-permute-done.17.refs_2_
  91.8 0.0 collective-permute-done.15.refs_0_
  91.8 2.1 %update.1 = (f32[768,256]{1,0:T(8,128)}, f32[768,256]{1,0:T(8,128)}, f32[6,128]{1,0:T(8,128)}, f32[6,128]{1,0:T(8,128)}) custom-call(s32[1]{0:T(128)} %bitcast.even_ref, f32[768,256]{1,0:T(8,128)S(1)} %copy-done.1, f32[768,256]{1,0:T(8,128)S(1)} %copy-done.3, f32[1,768]{1,0:T(1,128)S(1)} %reshape.34.row_acc, f32[1,768]{1,0:T(1,128)S(1)} %reshape.35.col_acc, ...), custom_call_target="tpu_custom_call" | custom-call | flops 1048576 | bytes 1024 | tf_op jit(solution)/shard_map/update/pallas_call | solution.py:268
  (23 shorter events, 0.1 us)
Async XLA Ops:
  0.6 1.1 %copy-start = (f32[768,256]{1,0:T(8,128)S(1)}, f32[768,256]{1,0:T(8,128)}, u32[]{:S(2)}) copy-start(f32[768,256]{1,0:T(8,128)} %row_emb.4) | copy-start | bytes 2359300
  1.8 1.1 %copy-start.2 = (f32[768,256]{1,0:T(8,128)S(1)}, f32[768,256]{1,0:T(8,128)}, u32[]{:S(2)}) copy-start(f32[768,256]{1,0:T(8,128)} %col_emb.4) | copy-start | bytes 2359300
  2.9 3.0 %copy-start.10 = (s32[12288]{0:T(1024)S(1)}, s32[12288]{0:T(1024)}, u32[]{:S(2)}) copy-start(s32[12288]{0:T(1024)} %param.11) | copy-start | bytes 147460
  3.0 20.1 %collective-permute-start.2 = (bf16[1536,256]{1,0:T(8,128)(2,1)S(1)}, bf16[1536,256]{1,0:T(8,128)(2,1)}, u32[]{:S(2)}, u32[]{:S(2)}) collective-permute-start(bf16[1536,256]{1,0:T(8,128)(2,1)S(1)} %rounded.1), channel_id=1, source_target_pairs={{0,2},{1,3},{2,4},{3,5},{4,6},{5,7},{6,8},{7,9},{8,10},{9,11},{10,... | collective-permute-start | bytes 2359304 | tf_op jit(solution)/shard_map/ppermute | solution.py:290
  5.9 5.7 %collective-permute-start = (f32[8,128]{1,0:T(8,128)S(1)}, f32[8,128]{1,0:T(8,128)S(1)}, u32[]{:S(2)}, u32[]{:S(2)}) collective-permute-start(f32[8,128]{1,0:T(8,128)S(1)} %bitcast_reduce_fusion), channel_id=1, source_target_pairs={{0,16},{16,0},{32,48},{48,32},{64,80},{80,64},{96,112},{112,96},{1... | collective-permute-start | bytes 12296 | tf_op jit(solution)/shard_map/ppermute | solution.py:306
  11.6 7.0 %collective-permute-start.1 = (f32[8,128]{1,0:T(8,128)S(1)}, f32[8,128]{1,0:T(8,128)S(1)}, u32[]{:S(2)}, u32[]{:S(2)}) collective-permute-start(f32[8,128]{1,0:T(8,128)S(1)} %add.49), channel_id=1, source_target_pairs={{0,32},{16,48},{32,0},{48,16},{64,96},{80,112},{96,64},{112,80},{1... | collective-permute-start | bytes 12296 | tf_op jit(solution)/shard_map/ppermute | solution.py:306
  13.9 24.2 %copy-start.1 = (f32[768,256]{1,0:T(8,128)S(1)}, f32[768,256]{1,0:T(8,128)}, u32[]{:S(2)}) copy-start(f32[768,256]{1,0:T(8,128)} %row_emb.4) | copy-start | bytes 2359300
  13.9 24.2 %copy-start.3 = (f32[768,256]{1,0:T(8,128)S(1)}, f32[768,256]{1,0:T(8,128)}, u32[]{:S(2)}) copy-start(f32[768,256]{1,0:T(8,128)} %col_emb.4) | copy-start | bytes 2359300
  18.6 4.4 %collective-permute-start.3 = (f32[8,128]{1,0:T(8,128)S(1)}, f32[8,128]{1,0:T(8,128)S(1)}, u32[]{:S(2)}, u32[]{:S(2)}) collective-permute-start(f32[8,128]{1,0:T(8,128)S(1)} %add.50), channel_id=1, source_target_pairs={{0,64},{16,80},{32,96},{48,112},{64,0},{80,16},{96,32},{112,48},{1... | collective-permute-start | bytes 12296 | tf_op jit(solution)/shard_map/ppermute | solution.py:306
  21.7 37.5 %collective-permute-start.8 = (bf16[1536,256]{1,0:T(8,128)(2,1)S(1)}, bf16[1536,256]{1,0:T(8,128)(2,1)}, u32[]{:S(2)}, u32[]{:S(2)}) collective-permute-start(bf16[1536,256]{1,0:T(8,128)(2,1)S(1)} %rounded.1), channel_id=1, source_target_pairs={{0,1},{2,3},{4,5},{6,7},{8,9},{10,11},{12,13},{14,15},{16,17},{18,... | collective-permute-start | bytes 2359304 | tf_op jit(solution)/shard_map/ppermute | solution.py:358
  23.0 23.0 %collective-permute-start.9 = (bf16[1536,256]{1,0:T(8,128)(2,1)}, bf16[1536,256]{1,0:T(8,128)(2,1)}, u32[]{:S(2)}, u32[]{:S(2)}) collective-permute-start(bf16[1536,256]{1,0:T(8,128)(2,1)} %collective-permute-done.2.refs_0_), channel_id=1, source_target_pairs={{0,1},{1,0},{2,3},{3,2},{4,5},{5,4},{6,7},{7,6},{8,9},{9,8},{10,11... | collective-permute-start | bytes 2359304 | tf_op jit(solution)/shard_map/ppermute | solution.py:290
  25.8 25.6 %collective-permute-start.5 = (bf16[1536,256]{1,0:T(8,128)(2,1)}, bf16[1536,256]{1,0:T(8,128)(2,1)S(1)}, u32[]{:S(2)}, u32[]{:S(2)}) collective-permute-start(bf16[1536,256]{1,0:T(8,128)(2,1)} %collective-permute-done.2.refs_0_), channel_id=1, source_target_pairs={{0,2},{1,3},{2,4},{3,5},{4,6},{5,7},{6,8},{7,9},{8,10},{9,11},{10,... | collective-permute-start | bytes 2359304 | tf_op jit(solution)/shard_map/ppermute | solution.py:290
  29.7 8.8 %collective-permute-start.4 = (f32[8,128]{1,0:T(8,128)S(1)}, f32[8,128]{1,0:T(8,128)S(1)}, u32[]{:S(2)}, u32[]{:S(2)}) collective-permute-start(f32[8,128]{1,0:T(8,128)S(1)} %add.51.total), channel_id=1, source_target_pairs={{0,128},{16,144},{32,160},{48,176},{64,192},{80,208},{96,224},{112... | collective-permute-start | bytes 12296 | tf_op jit(solution)/shard_map/ppermute | solution.py:306
  38.2 1.7 %copy-start.6 = (s32[768,768]{1,0:T(8,128)S(1)}, s32[768,768]{1,0:T(8,128)}, u32[]{:S(2)}) copy-start(s32[768,768]{1,0:T(8,128)} %get-tuple-element.67.laid) | copy-start | bytes 7077892
  38.2 1.7 %copy-start.9 = (f32[1,768]{1,0:T(1,128)S(1)}, f32[1,768]{1,0:T(1,128)}, u32[]{:S(2)}) copy-start(f32[1,768]{1,0:T(1,128)} %get-tuple-element.88.lm_cols) | copy-start | bytes 9220
  39.8 6.2 %copy-start.5 = (s32[768,768]{1,0:T(8,128)S(1)}, s32[768,768]{1,0:T(8,128)}, u32[]{:S(2)}) copy-start(s32[768,768]{1,0:T(8,128)} %get-tuple-element.66.laid) | copy-start | bytes 7077892
  39.8 6.2 %copy-start.8 = (f32[1,768]{1,0:T(1,128)S(1)}, f32[1,768]{1,0:T(1,128)}, u32[]{:S(2)}) copy-start(f32[1,768]{1,0:T(1,128)} %get-tuple-element.89.lm_cols) | copy-start | bytes 9220
  45.1 6.1 %collective-permute-start.10 = (bf16[256,768]{1,0:T(8,128)(2,1)S(1)}, bf16[256,768]{1,0:T(8,128)(2,1)S(1)}, u32[]{:S(2)}, u32[]{:S(2)}) collective-permute-start(bf16[256,768]{1,0:T(8,128)(2,1)S(1)} %get-tuple-element.72), channel_id=1, source_target_pairs={{0,1},{1,0},{2,3},{3,2},{4,5},{5,4},{6,7},{7,6},{8,9},{9,8},{10,11... | collective-permute-start | bytes 1179656 | tf_op jit(solution)/shard_map/ppermute | solution.py:290
  45.8 5.4 %collective-permute-start.11 = (bf16[256,768]{1,0:T(8,128)(2,1)S(1)}, bf16[256,768]{1,0:T(8,128)(2,1)S(1)}, u32[]{:S(2)}, u32[]{:S(2)}) collective-permute-start(bf16[256,768]{1,0:T(8,128)(2,1)S(1)} %get-tuple-element.73), channel_id=1, source_target_pairs={{0,1},{1,0},{2,3},{3,2},{4,5},{5,4},{6,7},{7,6},{8,9},{9,8},{10,11... | collective-permute-start | bytes 1179656 | tf_op jit(solution)/shard_map/ppermute | solution.py:290
  51.2 3.9 %copy-start.4 = (s32[768,768]{1,0:T(8,128)S(1)}, s32[768,768]{1,0:T(8,128)}, u32[]{:S(2)}) copy-start(s32[768,768]{1,0:T(8,128)} %get-tuple-element.65.laid) | copy-start | bytes 7077892
  51.3 39.9 %collective-permute-start.14 = (bf16[512,768]{1,0:T(8,128)(2,1)S(1)}, bf16[512,768]{1,0:T(8,128)(2,1)S(1)}, u32[]{:S(2)}, u32[]{:S(2)}) collective-permute-start(bf16[512,768]{1,0:T(8,128)(2,1)S(1)} %join.2), channel_id=1, source_target_pairs={{0,15},{1,14},{2,1},{3,0},{4,3},{5,2},{6,5},{7,4},{8,7},{9,6},{10,... | collective-permute-start | bytes 2359304 | tf_op jit(solution)/shard_map/ppermute | solution.py:290
  51.5 8.3 %collective-permute-start.6 = (bf16[768,256]{1,0:T(8,128)(2,1)S(1)}, bf16[768,256]{1,0:T(8,128)(2,1)S(1)}, u32[]{:S(2)}, u32[]{:S(2)}) collective-permute-start(bf16[768,256]{1,0:T(8,128)(2,1)S(1)} %get-tuple-element.87), channel_id=1, source_target_pairs={{1,0},{3,2},{5,4},{7,6},{9,8},{11,10},{13,12},{15,14},{17,16},{19,... | collective-permute-start | bytes 1179656 | tf_op jit(solution)/shard_map/ppermute | solution.py:359
  53.8 6.0 %collective-permute-start.7 = (bf16[768,256]{1,0:T(8,128)(2,1)S(1)}, bf16[768,256]{1,0:T(8,128)(2,1)S(1)}, u32[]{:S(2)}, u32[]{:S(2)}) collective-permute-start(bf16[768,256]{1,0:T(8,128)(2,1)S(1)} %get-tuple-element.86), channel_id=1, source_target_pairs={{1,0},{3,2},{5,4},{7,6},{9,8},{11,10},{13,12},{15,14},{17,16},{19,... | collective-permute-start | bytes 1179656 | tf_op jit(solution)/shard_map/ppermute | solution.py:359
  55.1 4.7 %copy-start.11 = (f32[768]{0:T(1024)S(1)}, f32[768]{0:T(1024)}, u32[]{:S(2)}) copy-start(f32[768]{0:T(1024)} %param.8) | copy-start | bytes 9220
  55.1 4.6 %copy-start.12 = (f32[768]{0:T(1024)S(1)}, f32[768]{0:T(1024)}, u32[]{:S(2)}) copy-start(f32[768]{0:T(1024)} %param.9) | copy-start | bytes 9220
  55.1 4.7 %copy-start.7 = (s32[768,768]{1,0:T(8,128)S(1)}, s32[768,768]{1,0:T(8,128)}, u32[]{:S(2)}) copy-start(s32[768,768]{1,0:T(8,128)} %get-tuple-element.54.laid) | copy-start | bytes 7077892
  59.2 6.4 %collective-permute-start.12 = (bf16[256,768]{1,0:T(8,128)(2,1)S(1)}, bf16[256,768]{1,0:T(8,128)(2,1)S(1)}, u32[]{:S(2)}, u32[]{:S(2)}) collective-permute-start(bf16[256,768]{1,0:T(8,128)(2,1)S(1)} %get-tuple-element.79), channel_id=1, source_target_pairs={{0,1},{1,0},{2,3},{3,2},{4,5},{5,4},{6,7},{7,6},{8,9},{9,8},{10,11... | collective-permute-start | bytes 1179656 | tf_op jit(solution)/shard_map/ppermute | solution.py:290
  59.3 6.3 %collective-permute-start.13 = (bf16[256,768]{1,0:T(8,128)(2,1)S(1)}, bf16[256,768]{1,0:T(8,128)(2,1)S(1)}, u32[]{:S(2)}, u32[]{:S(2)}) collective-permute-start(bf16[256,768]{1,0:T(8,128)(2,1)S(1)} %get-tuple-element.80), channel_id=1, source_target_pairs={{0,1},{1,0},{2,3},{3,2},{4,5},{5,4},{6,7},{7,6},{8,9},{9,8},{10,11... | collective-permute-start | bytes 1179656 | tf_op jit(solution)/shard_map/ppermute | solution.py:290
  65.0 26.7 %collective-permute-start.16 = (bf16[256,768]{1,0:T(8,128)(2,1)S(1)}, bf16[256,768]{1,0:T(8,128)(2,1)S(1)}, u32[]{:S(2)}, u32[]{:S(2)}) collective-permute-start(bf16[256,768]{1,0:T(8,128)(2,1)S(1)} %get-tuple-element.77.row_here), channel_id=1, source_target_pairs={{0,1},{1,0},{2,3},{3,2},{4,5},{5,4},{6,7},{7,6},{8,9},{9,8},{10,11... | collective-permute-start | bytes 1179656 | tf_op jit(solution)/shard_map/ppermute | solution.py:290
  65.4 26.3 %collective-permute-start.17 = (bf16[256,768]{1,0:T(8,128)(2,1)S(1)}, bf16[256,768]{1,0:T(8,128)(2,1)S(1)}, u32[]{:S(2)}, u32[]{:S(2)}) collective-permute-start(bf16[256,768]{1,0:T(8,128)(2,1)S(1)} %get-tuple-element.78.col_here), channel_id=1, source_target_pairs={{0,1},{1,0},{2,3},{3,2},{4,5},{5,4},{6,7},{7,6},{8,9},{9,8},{10,11... | collective-permute-start | bytes 1179656 | tf_op jit(solution)/shard_map/ppermute | solution.py:290
  65.7 26.1 %collective-permute-start.15 = (bf16[512,768]{1,0:T(8,128)(2,1)S(1)}, bf16[512,768]{1,0:T(8,128)(2,1)S(1)}, u32[]{:S(2)}, u32[]{:S(2)}) collective-permute-start(bf16[512,768]{1,0:T(8,128)(2,1)S(1)} %join.3), channel_id=1, source_target_pairs={{0,13},{1,12},{2,15},{3,14},{4,1},{5,0},{6,3},{7,2},{8,5},{9,4},{1... | collective-permute-start | bytes 2359304 | tf_op jit(solution)/shard_map/ppermute | solution.py:290
where the time goes:
time: 94.3 us; the launch traced here: 93.8 us
  Pallas kernels  31.9 us (34%)
  starting transfers between devices  28.9 us (31%)
  waiting for transfers between devices  25.5 us (27%)
  local copies, waits for them, and re-layouts  5.17 us (5%)
  other arithmetic  1.21 us (1%)
  between operations  1.13 us (1%)
    ppermute x11, waiting for transfers between devices, moved(): return lax.ppermute(array, 'blk', route)  25.5 us
    pallas_call x4, Pallas kernels, tile(): pl.pallas_call(functools.partial(tile_kernel, start=start, span=span, row...  19.6 us
    ppermute x4, starting transfers between devices, from_reach(): return lax.ppermute(total, 'slab', [(i, i ^ reach) for i in range(slabs)])  12.3 us
    ppermute x11, starting transfers between devices, moved(): return lax.ppermute(array, 'blk', route)  11.7 us
    pallas_call x2, Pallas kernels, lay(): pl.pallas_call(lay_kernel, in_specs=[SMEM, ANY], out_specs=[ANY] * steps,...  9.3 us
    ppermute x2, starting transfers between devices, per_device(): lax.ppermute(far_in[i * block:(i + 1) * block], 'blk', to_even)  3.61 us
    unnamed x26, local copies, waits for them, and re-layouts  3.56 us
    pallas_call x1, Pallas kernels, update(): pl.pallas_call(update_kernel, in_specs=[SMEM] + [VMEM] * (5 + 3 * len(far...  2.06 us
  transfers between devices with their start and end apart: 18, of which 1 were waited for; matrix products, arithmetic and copies ran while one was open for 3% of the time, Pallas kernels for 32%

commit v1 on v0

--- a/solution.py
+++ b/solution.py
@@ -41,34 +41,40 @@
     )(row_emb, col_emb)
 
 
-def turned_kernel(row_emb, col_emb, own_half, own_t):
+def turned_kernel(row_emb, col_emb, *refs):
+    logs, (own_half, own_t, lm_rows), lm_cols = refs[:5], refs[5:8], refs[8:]
     block, width = row_emb.shape
     for side, emb in enumerate((row_emb, col_emb)):
         values = emb[...].astype(bf16)
         own_half[pl.ds(side * block, block), :] = values * bf16(0.5)
         own_t[pl.ds(side * width, width), :] = values.T
-
-
-def turned(row_emb, col_emb):
+    lm_rows[...] = jnp.broadcast_to(logs[0][...], (8, block)).T[:, :1]
+    for log, out in zip(logs[1:], lm_cols):
+        out[...] = log[...]
+
+
+def turned(row_emb, col_emb, logs):
     block, width = row_emb.shape
     return pl.pallas_call(
         turned_kernel,
-        in_specs=[VMEM] * 2,
-        out_specs=[VMEM] * 2,
+        in_specs=[VMEM] * 7,
+        out_specs=[VMEM] * 7,
         out_shape=[
             jax.ShapeDtypeStruct((2 * block, width), bf16),
             jax.ShapeDtypeStruct((2 * width, block), bf16),
-        ],
-        compiler_params=pltpu.CompilerParams(vmem_limit_bytes=8 << 20),
+            jax.ShapeDtypeStruct((block, 1), f32),
+        ]
+        + [jax.ShapeDtypeStruct((1, block), f32)] * 4,
+        compiler_params=pltpu.CompilerParams(vmem_limit_bytes=12 << 20),
         cost_estimate=SMALL,
         name="turned",
-    )(row_emb, col_emb)
-
-
-def lay_kernel(k_ref, counts, *refs):
+    )(row_emb, col_emb, *logs)
+
+
+def lay_kernel(k_ref, counts, *refs, base):
     outs, held, sems_in, sems_out = refs[:-3], refs[-3], refs[-2], refs[-1]
     copies = [
-        pltpu.make_async_copy(counts.at[:, k_ref[i], :], held.at[i], sems_in.at[i])
+        pltpu.make_async_copy(counts.at[:, k_ref[base + i], :], held.at[i], sems_in.at[i])
         for i in range(len(outs))
     ]
     for copy in copies:
@@ -82,11 +88,10 @@
         copy.wait()
 
 
-def lay(offsets, counts):
+def lay(offsets, counts, base, steps):
     block, _, width = counts.shape
-    steps = len(offsets)
-    return pl.pallas_call(
-        lay_kernel,
+    return pl.pallas_call(
+        functools.partial(lay_kernel, base=base),
         in_specs=[SMEM, ANY],
         out_specs=[ANY] * steps,
         out_shape=[jax.ShapeDtypeStruct((block, width), jnp.int32)] * steps,
@@ -98,17 +103,18 @@
         compiler_params=pltpu.CompilerParams(vmem_limit_bytes=56 << 20),
         cost_estimate=SMALL,
         name="lay",
-    )(jnp.stack(offsets), counts)
+    )(offsets, counts)
 
 
 def tile_kernel(
     even_ref, laid, total, more_total, lm_rows, lm_cols, own_half, own_t, *refs,
-    start, span, rows, cols, kind,
+    start, span, rows, cols, kind, first,
 ):
     block = own_half.shape[0] // 2
     width = own_half.shape[1]
     parts = refs[: {"whole": 1, "halves": 2, "either": 3}[kind]]
-    acc_in, acc, back_row, back_col, tiles, sems = refs[len(parts) :]
+    refs = refs[len(parts) :]
+    acc_in, (acc, back_row, back_col, tiles, sems) = (None, refs) if first else (refs[0], refs[1:])
     even = even_ref[0] == 1
 
     def partner(side, j):
@@ -154,7 +160,8 @@
                 differ = logits - goal
                 grad = jnp.where(positive, sure * differ, 0.5 * jnp.tanh(differ) + 0.5).astype(bf16)
                 source = acc_in if j == 0 else acc
-                acc[at, :] = source[at, :] + jnp.dot(grad, seen, preferred_element_type=f32)
+                own = jnp.dot(grad, seen, preferred_element_type=f32)
+                acc[at, :] = own if source is None else source[at, :] + own
                 more = jnp.dot(
                     own_t[pl.ds(side * width, width), mine], grad, preferred_element_type=f32
                 )
@@ -167,9 +174,10 @@
     block, width = own_half.shape[0] // 2, own_half.shape[1]
     cols = min(cols, span)
     kind = ("whole", "halves", "either")[len(parts) - 1]
-    return pl.pallas_call(
-        functools.partial(tile_kernel, start=start, span=span, rows=rows, cols=cols, kind=kind),
-        in_specs=[SMEM, ANY] + [VMEM] * (7 + len(parts)),
+    first = acc is None
+    return pl.pallas_call(
+        functools.partial(tile_kernel, start=start, span=span, rows=rows, cols=cols, kind=kind, first=first),
+        in_specs=[SMEM, ANY] + [VMEM] * (7 - first + len(parts)),
         out_specs=[VMEM] * 3,
         out_shape=[jax.ShapeDtypeStruct((2 * block, width), f32)]
         + [jax.ShapeDtypeStruct((width, span), bf16)] * 2,
@@ -177,11 +185,11 @@
             pltpu.VMEM((block, span), jnp.int32),
             pltpu.SemaphoreType.DMA((span // cols,)),
         ],
-        input_output_aliases={8 + len(parts): 0},
+        input_output_aliases={} if first else {8 + len(parts): 0},
         compiler_params=pltpu.CompilerParams(vmem_limit_bytes=GRANT),
         cost_estimate=SMALL,
         name="tile",
-    )(even, laid, *totals, lm_rows, lm_cols, own_half, own_t, *parts, acc)
+    )(even, laid, *totals, lm_rows, lm_cols, own_half, own_t, *parts, *([] if first else [acc]))
 
 
 def join_kernel(even_ref, row_here, col_here, row_there, col_there, out):
@@ -302,42 +310,49 @@
     total = jnp.sum(marg_f.reshape(-1, 8, 128), axis=0)
     slabs = lax.axis_size("slab")
 
+    shifts = [jnp.int32(2), shift_near, jnp.int32(4), shift_far]
+    offsets = [shift - 1 for shift in shifts]
+    offsets = jnp.stack(offsets)
+
     def from_reach(total, reach):
         return lax.ppermute(total, "slab", [(i, i ^ reach) for i in range(slabs)])
 
     there = from_reach(total, 1)
     (piece,) = rounded(row_emb, col_emb, (block,))
     near_in = moved(piece, 2)
-    shifts = [jnp.int32(2), shift_near, jnp.int32(4), shift_far]
-    offsets = [shift - 1 for shift in shifts]
-    *first, piece = lax.optimization_barrier((*offsets[:2], piece))
-    laid = lay(first, counts)
+    to_even = [(i, i - 1) for i in range(1, cycle, 2)]
+    to_odd = [(i, i + 1) for i in range(0, cycle, 2)]
+    offsets, piece = lax.optimization_barrier((offsets, piece))
+    laid = lay(offsets, counts, 0, 2)
     *laid, there = lax.optimization_barrier((*laid, there))
     total = total + there
     there = from_reach(total, 2)
-    *second, total = lax.optimization_barrier((*offsets[2:], total))
-    later = lay(second, counts)
-    *later, there = lax.optimization_barrier((*later, there))
-    laid = [*laid, *later]
+    offsets, total = lax.optimization_barrier((offsets, total))
+    beside = lax.ppermute(piece, "blk", to_odd)
+    laid += lay(offsets, counts, 2, 2)
+    *laid, beside, there = lax.optimization_barrier((*laid, beside, there))
     total = total + there
     there = from_reach(total, 4)
-    total = total + there
-    there = from_reach(total, 8)
-    near_in, total = lax.optimization_barrier((near_in, total))
-    far_in = moved(near_in if RELAY else piece, 2 if RELAY else 4)
-    row_again, col_again, total = lax.optimization_barrier((row_emb, col_emb, total))
-    own_half, own_t = turned(row_again, col_again)
-    totals = (total, there)
+    row_again, col_again, marg_f, total = lax.optimization_barrier((row_emb, col_emb, marg_f, total))
     log_marg = jnp.log(marg_f).reshape(cycle, 1, block)
 
     def log_marg_of(place):
         return lax.dynamic_index_in_dim(log_marg, place % cycle, keepdims=False)
 
-    lm_rows = log_marg_of(me).reshape(block, 1)
-    acc = jnp.zeros((2 * block, width), f32)
+    logs = [log_marg_of(me)] + [log_marg_of(me - shift) for shift in shifts]
+    own_half, own_t, lm_rows, *lm_cols = turned(row_again, col_again, logs)
+    own_half, own_t, lm_rows, there, *lm_cols = lax.optimization_barrier(
+        (own_half, own_t, lm_rows, there, *lm_cols)
+    )
+    total = total + there
+    there = from_reach(total, 12)
+    near_in, there = lax.optimization_barrier((near_in, there))
+    far_in = moved(near_in, 2)
+    totals = (total, there)
+
     def tiles(slot, parts, acc, start, span):
         acc, *backs = tile(
-            even, laid[slot], totals, lm_rows, log_marg_of(me - shifts[slot]), own_half, own_t, parts,
+            even, laid[slot], totals, lm_rows, lm_cols[slot], own_half, own_t, parts,
             acc, start, span,
         )
         return acc, backs
@@ -346,16 +361,13 @@
         return [function(array) for array in arrays]
 
     other = swapped(near_in)
-    acc, back_two = tiles(0, [near_in], acc, 0, block)
+    acc, back_two = tiles(0, [near_in], None, 0, block)
     from_other = both(swapped, back_two)
     acc, back_near = tiles(1, [other], acc, 0, block)
     joined = join(jnp.ones_like(even), back_near, from_other)
     near_out = [moved(joined, -1, -3)]
     acc, joined = lax.optimization_barrier((acc, joined))
     chip_out, far_out = [], []
-    to_even = [(i, i - 1) for i in range(1, cycle, 2)]
-    to_odd = [(i, i + 1) for i in range(0, cycle, 2)]
-    beside = lax.ppermute(piece, "blk", to_odd)
     other = [lax.ppermute(far_in[i * block : (i + 1) * block], "blk", to_even) for i in range(2)]
     for start, span in zip(starts_of(FAR), FAR):
         acc, back_four = tiles(2, [far_in], acc, start, span)

time: 94.3 us -> 93.2 us (0.988); the launches traced: 93.8 us -> 91.5 us
  starting transfers between devices: 28.9 us -> 26.5 us
  waiting for transfers between devices: 25.5 us -> 27.8 us
  Pallas kernels: 31.9 us -> 30.7 us
    ppermute x4, starting transfers between devices: 12.3 us -> 9.82 us  [from_reach(): return lax.ppermute(total, 'slab', [(i, i ^ reach) for i in range(slabs)])]
    ppermute x4, waiting for transfers between devices: 0.01 us -> 1.52 us  [from_reach(): return lax.ppermute(total, 'slab', [(i, i ^ reach) for i in range(slabs)])]
    pallas_call x4, Pallas kernels: 19.6 us -> 18.3 us  [tile(): pl.pallas_call(functools.partial(tile_kernel, start=start, span=span, row...]
    unnamed x26 -> x34, local copies, waits for them, and re-layouts: 3.56 us -> 4.71 us
  transfers between devices with their start and end apart: 18 -> 18, of which waited for: 1 -> 5; matrix products, arithmetic and copies ran while one was open for 3% -> 0% of each run, Pallas kernels for 32% -> 31%
where the time goes in v1:
time: 93.2 us; the launch traced here: 91.5 us
  Pallas kernels  30.7 us (33%)
  waiting for transfers between devices  27.8 us (30%)
  starting transfers between devices  26.5 us (28%)
  local copies, waits for them, and re-layouts  4.8 us (5%)
  between operations  1 us (1%)
    ppermute x11, waiting for transfers between devices, moved(): return lax.ppermute(array, 'blk', route)  26.3 us
    pallas_call x4, Pallas kernels, tile(): pl.pallas_call(functools.partial(tile_kernel, start=start, span=span, row...  18.3 us
    ppermute x11, starting transfers between devices, moved(): return lax.ppermute(array, 'blk', route)  11.4 us
    ppermute x4, starting transfers between devices, from_reach(): return lax.ppermute(total, 'slab', [(i, i ^ reach) for i in range(slabs)])  9.82 us
    pallas_call x2, Pallas kernels, lay(): pl.pallas_call(functools.partial(lay_kernel, base=base), in_specs=[SMEM,...  9.28 us
    unnamed x34, local copies, waits for them, and re-layouts  4.71 us
    ppermute x2, starting transfers between devices, per_device(): lax.ppermute(far_in[i * block:(i + 1) * block], 'blk', to_even)  4.03 us
    pallas_call x1, Pallas kernels, update(): pl.pallas_call(update_kernel, in_specs=[SMEM] + [VMEM] * (5 + 3 * len(far...  2.04 us
  transfers between devices with their start and end apart: 18, of which 5 were waited for; matrix products, arithmetic and copies ran while one was open for 0% of the time, Pallas kernels for 31%

profile of v1, /device:TPU:7, one launch (start us, length us, event | category | flops | bytes accessed | tf_op | source)
XLA Modules:
  0.0 91.5 jit_solution(8994576520433536568)
XLA Ops:
  0.6 0.0 copy-start
  0.7 1.1 %copy-done = f32[768,256]{1,0:T(8,128)S(1)} copy-done((f32[768,256]{1,0:T(8,128)S(1)}, f32[768,256]{1,0:T(8,128)}, u32[]{:S(2)}) %copy-start) | copy-done | bytes 786456
  1.8 1.1 %copy-done.3 = f32[768,256]{1,0:T(8,128)S(1)} copy-done((f32[768,256]{1,0:T(8,128)S(1)}, f32[768,256]{1,0:T(8,128)}, u32[]{:S(2)}) %copy-start.3) | copy-done | bytes 786456
  2.9 0.1 rounded.1
  3.0 0.6 pad_add_fusion.k_ref
  3.6 1.3 %collective-permute-start.1 = (bf16[1536,256]{1,0:T(8,128)(2,1)S(1)}, bf16[1536,256]{1,0:T(8,128)(2,1)S(1)}, u32[]{:S(2)}, u32[]{:S(2)}) collective-permute-start(bf16[1536,256]{1,0:T(8,128)(2,1)S(1)} %rounded.1), channel_id=1, source_target_pairs={{0,1},{2,3},{4,5},{6,7},{8,9},{10,11},{12,13},{14,15},{16,17},{18,... | collective-permute-start | bytes 2359304 | tf_op jit(solution)/shard_map/ppermute | solution.py:331
  4.9 2.9 %collective-permute-start.4 = (bf16[1536,256]{1,0:T(8,128)(2,1)S(1)}, bf16[1536,256]{1,0:T(8,128)(2,1)}, u32[]{:S(2)}, u32[]{:S(2)}) collective-permute-start(bf16[1536,256]{1,0:T(8,128)(2,1)S(1)} %rounded.1), channel_id=1, source_target_pairs={{0,2},{1,3},{2,4},{3,5},{4,6},{5,7},{6,8},{7,9},{8,10},{9,11},{10,... | collective-permute-start | bytes 2359304 | tf_op jit(solution)/shard_map/ppermute | solution.py:298
  7.8 0.0 copy-done.14
  7.8 0.5 collective-permute-start
  8.3 4.6 %lay.2 = (s32[768,768]{1,0:T(8,128)}, s32[768,768]{1,0:T(8,128)}) custom-call(s32[4]{0:T(128)} %pad_add_fusion.k_ref, s32[768,4,768]{2,1,0:T(4,128)} %counts.3), custom_call_target="tpu_custom_call" | custom-call | flops 1048576 | bytes 1024 | tf_op jit(solution)/shard_map/lay/pallas_call | solution.py:93
  12.9 0.0 collective-permute-done
  12.9 1.7 %collective-permute-start.2 = (f32[8,128]{1,0:T(8,128)S(1)}, f32[8,128]{1,0:T(8,128)S(1)}, u32[]{:S(2)}, u32[]{:S(2)}) collective-permute-start(f32[8,128]{1,0:T(8,128)S(1)} %add.49), channel_id=1, source_target_pairs={{0,32},{16,48},{32,0},{48,16},{64,96},{80,112},{96,64},{112,80},{1... | collective-permute-start | bytes 12296 | tf_op jit(solution)/shard_map/ppermute | solution.py:318
  14.6 4.7 %lay.3 = (s32[768,768]{1,0:T(8,128)}, s32[768,768]{1,0:T(8,128)}) custom-call(s32[4]{0:T(128)} %pad_add_fusion.k_ref, s32[768,4,768]{2,1,0:T(4,128)} %counts.3), custom_call_target="tpu_custom_call" | custom-call | flops 1048576 | bytes 1024 | tf_op jit(solution)/shard_map/lay/pallas_call | solution.py:93
  19.3 0.0 collective-permute-done.2
  19.4 0.0 collective-permute-done.1.refs_2_
  19.4 3.1 %collective-permute-start.3 = (f32[8,128]{1,0:T(8,128)S(1)}, f32[8,128]{1,0:T(8,128)S(1)}, u32[]{:S(2)}, u32[]{:S(2)}) collective-permute-start(f32[8,128]{1,0:T(8,128)S(1)} %add.50), channel_id=1, source_target_pairs={{0,64},{16,80},{32,96},{48,112},{64,0},{80,16},{96,32},{112,48},{1... | collective-permute-start | bytes 12296 | tf_op jit(solution)/shard_map/ppermute | solution.py:318
  22.5 0.4 turned.1
  22.9 0.0 copy-start.10
  22.9 0.0 copy-start.12
  22.9 0.5 collective-permute-done.3
  23.5 0.0 copy-done.10
  23.5 0.0 copy-done.12
  23.5 4.5 %collective-permute-start.5 = (f32[8,128]{1,0:T(8,128)S(1)}, f32[8,128]{1,0:T(8,128)S(1)}, u32[]{:S(2)}, u32[]{:S(2)}) collective-permute-start(f32[8,128]{1,0:T(8,128)S(1)} %add.61.total), channel_id=1, source_target_pairs={{0,192},{16,208},{32,224},{48,240},{64,128},{80,144},{96,160},{112... | collective-permute-start | bytes 12296 | tf_op jit(solution)/shard_map/ppermute | solution.py:318
  28.0 0.0 collective-permute-done.4.refs_0_
  28.0 1.0 %collective-permute-done.5.more_total = f32[8,128]{1,0:T(8,128)S(1)} collective-permute-done((f32[8,128]{1,0:T(8,128)S(1)}, f32[8,128]{1,0:T(8,128)S(1)}, u32[]{:S(2)}, u32[]{:S(2)}) %collective-permute-start.5) | collective-permute-done | bytes 4128 | tf_op jit(solution)/shard_map/ppermute | solution.py:318
  29.0 4.0 %collective-permute-start.9 = (bf16[1536,256]{1,0:T(8,128)(2,1)}, bf16[1536,256]{1,0:T(8,128)(2,1)}, u32[]{:S(2)}, u32[]{:S(2)}) collective-permute-start(bf16[1536,256]{1,0:T(8,128)(2,1)} %collective-permute-done.4.refs_0_), channel_id=1, source_target_pairs={{0,1},{1,0},{2,3},{3,2},{4,5},{5,4},{6,7},{7,6},{8,9},{9,8},{10,11... | collective-permute-start | bytes 2359304 | tf_op jit(solution)/shard_map/ppermute | solution.py:298
  33.1 1.8 %collective-permute-start.6 = (bf16[1536,256]{1,0:T(8,128)(2,1)}, bf16[1536,256]{1,0:T(8,128)(2,1)S(1)}, u32[]{:S(2)}, u32[]{:S(2)}) collective-permute-start(bf16[1536,256]{1,0:T(8,128)(2,1)} %collective-permute-done.4.refs_0_), channel_id=1, source_target_pairs={{0,2},{1,3},{2,4},{3,5},{4,6},{5,7},{6,8},{7,9},{8,10},{9,11},{10,... | collective-permute-start | bytes 2359304 | tf_op jit(solution)/shard_map/ppermute | solution.py:298
  34.9 1.7 %copy-done.8 = s32[768,768]{1,0:T(8,128)S(1)} copy-done((s32[768,768]{1,0:T(8,128)S(1)}, s32[768,768]{1,0:T(8,128)}, u32[]{:S(2)}) %copy-start.8) | copy-done | bytes 2359320
  36.6 0.7 copy-done.13
  37.2 5.1 %tile.4 = (f32[1536,256]{1,0:T(8,128)S(1)}, bf16[256,768]{1,0:T(8,128)(2,1)S(1)}, bf16[256,768]{1,0:T(8,128)(2,1)S(1)}) custom-call(s32[1]{0:T(128)} %bitcast.even_ref, s32[768,768]{1,0:T(8,128)S(1)} %copy-done.8, f32[8,128]{1,0:T(8,128)S(1)} %add.61.total, f32[8,128]{1,0:T(8,128)S(1)} %collective-permute-done.5.more_total, ...), custom_call_target="tpu_custom_call" | custom-call | flops 1048576 | bytes 1024 | tf_op jit(solution)/shard_map/tile/pallas_call | solution.py:178
  42.4 0.4 collective-permute-start.10
  42.8 0.3 collective-permute-start.11
  43.1 0.0 collective-permute-done.9.refs_0_
  43.1 5.1 %tile.5 = (f32[1536,256]{1,0:T(8,128)S(1)}, bf16[256,768]{1,0:T(8,128)(2,1)S(1)}, bf16[256,768]{1,0:T(8,128)(2,1)S(1)}) custom-call(s32[1]{0:T(128)} %bitcast.even_ref, s32[768,768]{1,0:T(8,128)S(1)} %copy-done.6, f32[8,128]{1,0:T(8,128)S(1)} %add.61.total, f32[8,128]{1,0:T(8,128)S(1)} %collective-permute-done.5.more_total, ...), custom_call_target="tpu_custom_call", output_to_operand_aliasing={{0}: (9, {})} | custom-call | flops 1048576 | bytes 1024 | tf_op jit(solution)/shard_map/tile/pallas_call | solution.py:178
  48.2 0.0 collective-permute-done.10.row_there
  48.2 0.0 collective-permute-done.11.col_there
  48.2 0.1 join.2
  48.3 0.1 collective-permute-start.14
  48.4 4.0 %collective-permute-done.6.refs_0_ = bf16[1536,256]{1,0:T(8,128)(2,1)S(1)} collective-permute-done((bf16[1536,256]{1,0:T(8,128)(2,1)}, bf16[1536,256]{1,0:T(8,128)(2,1)S(1)}, u32[]{:S(2)}, u32[]{:S(2)}) %collective-permute-start.6) | collective-permute-done | bytes 786464 | tf_op jit(solution)/shard_map/ppermute | solution.py:298
  52.5 0.1 fusion
  52.5 2.7 %collective-permute-start.7 = (bf16[768,256]{1,0:T(8,128)(2,1)S(1)}, bf16[768,256]{1,0:T(8,128)(2,1)S(1)}, u32[]{:S(2)}, u32[]{:S(2)}) collective-permute-start(bf16[768,256]{1,0:T(8,128)(2,1)S(1)} %get-tuple-element.117), channel_id=1, source_target_pairs={{1,0},{3,2},{5,4},{7,6},{9,8},{11,10},{13,12},{15,14},{17,16},{19,... | collective-permute-start | bytes 1179656 | tf_op jit(solution)/shard_map/ppermute | solution.py:371
  55.2 1.3 %collective-permute-start.8 = (bf16[768,256]{1,0:T(8,128)(2,1)S(1)}, bf16[768,256]{1,0:T(8,128)(2,1)S(1)}, u32[]{:S(2)}, u32[]{:S(2)}) collective-permute-start(bf16[768,256]{1,0:T(8,128)(2,1)S(1)} %get-tuple-element.116), channel_id=1, source_target_pairs={{1,0},{3,2},{5,4},{7,6},{9,8},{11,10},{13,12},{15,14},{17,16},{19,... | collective-permute-start | bytes 1179656 | tf_op jit(solution)/shard_map/ppermute | solution.py:371
  56.6 0.0 copy-done.7
  56.6 0.0 copy-start.15
  56.6 0.0 copy-start.16
  56.6 4.0 %tile.6 = (f32[1536,256]{1,0:T(8,128)S(1)}, bf16[256,768]{1,0:T(8,128)(2,1)S(1)}, bf16[256,768]{1,0:T(8,128)(2,1)S(1)}) custom-call(s32[1]{0:T(128)} %bitcast.even_ref, s32[768,768]{1,0:T(8,128)S(1)} %copy-done.7, f32[8,128]{1,0:T(8,128)S(1)} %add.61.total, f32[8,128]{1,0:T(8,128)S(1)} %collective-permute-done.5.more_total, ...), custom_call_target="tpu_custom_call", output_to_operand_aliasing={{0}: (9, {})} | custom-call | flops 1048576 | bytes 1024 | tf_op jit(solution)/shard_map/tile/pallas_call | solution.py:178
  60.6 0.1 collective-permute-start.12
  60.7 0.5 collective-permute-start.13
  61.2 0.0 collective-permute-done.7.refs_0_
  61.3 0.0 collective-permute-done.8.refs_1_
  61.3 4.0 %tile.7 = (f32[1536,256]{1,0:T(8,128)S(1)}, bf16[256,768]{1,0:T(8,128)(2,1)S(1)}, bf16[256,768]{1,0:T(8,128)(2,1)S(1)}) custom-call(s32[1]{0:T(128)} %bitcast.even_ref, s32[768,768]{1,0:T(8,128)S(1)} %copy-done.9, f32[8,128]{1,0:T(8,128)S(1)} %add.61.total, f32[8,128]{1,0:T(8,128)S(1)} %collective-permute-done.5.more_total, ...), custom_call_target="tpu_custom_call", output_to_operand_aliasing={{0}: (11, {})} | custom-call | flops 1048576 | bytes 1024 | tf_op jit(solution)/shard_map/tile/pallas_call | solution.py:178
  65.3 0.4 collective-permute-start.16
  65.7 0.2 collective-permute-start.17
  65.9 0.0 collective-permute-done.12.row_there
  65.9 0.0 collective-permute-done.13.col_there
  65.9 0.1 join.3
  66.0 0.7 collective-permute-start.15
  66.7 4.7 %collective-permute-done.14.refs_0_ = bf16[512,768]{1,0:T(8,128)(2,1)S(1)} collective-permute-done((bf16[512,768]{1,0:T(8,128)(2,1)S(1)}, bf16[512,768]{1,0:T(8,128)(2,1)S(1)}, u32[]{:S(2)}, u32[]{:S(2)}) %collective-permute-start.14) | collective-permute-done | bytes 786464 | tf_op jit(solution)/shard_map/ppermute | solution.py:298
  71.4 0.5 gather_up.1.grads
  71.9 0.0 collective-permute-done.16.refs_1_
  71.9 0.0 collective-permute-done.17.refs_2_
  71.9 17.5 %collective-permute-done.15.refs_0_ = bf16[512,768]{1,0:T(8,128)(2,1)S(1)} collective-permute-done((bf16[512,768]{1,0:T(8,128)(2,1)S(1)}, bf16[512,768]{1,0:T(8,128)(2,1)S(1)}, u32[]{:S(2)}, u32[]{:S(2)}) %collective-permute-start.15) | collective-permute-done | bytes 786464 | tf_op jit(solution)/shard_map/ppermute | solution.py:298
  89.5 0.0 copy-done.5
  89.5 2.0 %update.1 = (f32[768,256]{1,0:T(8,128)}, f32[768,256]{1,0:T(8,128)}, f32[6,128]{1,0:T(8,128)}, f32[6,128]{1,0:T(8,128)}) custom-call(s32[1]{0:T(128)} %bitcast.even_ref, f32[768,256]{1,0:T(8,128)S(1)} %copy-done.2, f32[768,256]{1,0:T(8,128)S(1)} %copy-done.5, f32[1,768]{1,0:T(1,128)S(1)} %reshape.30.row_acc, f32[1,768]{1,0:T(1,128)S(1)} %reshape.31.col_acc, ...), custom_call_target="tpu_custom_call" | custom-call | flops 1048576 | bytes 1024 | tf_op jit(solution)/shard_map/update/pallas_call | solution.py:276
  (29 shorter events, 0.1 us)
Async XLA Ops:
  0.6 1.1 %copy-start = (f32[768,256]{1,0:T(8,128)S(1)}, f32[768,256]{1,0:T(8,128)}, u32[]{:S(2)}) copy-start(f32[768,256]{1,0:T(8,128)} %row_emb.4) | copy-start | bytes 2359300
  1.8 1.1 %copy-start.3 = (f32[768,256]{1,0:T(8,128)S(1)}, f32[768,256]{1,0:T(8,128)}, u32[]{:S(2)}) copy-start(f32[768,256]{1,0:T(8,128)} %col_emb.4) | copy-start | bytes 2359300
  2.9 4.9 %copy-start.14 = (s32[12288]{0:T(1024)S(1)}, s32[12288]{0:T(1024)}, u32[]{:S(2)}) copy-start(s32[12288]{0:T(1024)} %param.11) | copy-start | bytes 147460
  3.6 15.8 %collective-permute-start.1 = (bf16[1536,256]{1,0:T(8,128)(2,1)S(1)}, bf16[1536,256]{1,0:T(8,128)(2,1)S(1)}, u32[]{:S(2)}, u32[]{:S(2)}) collective-permute-start(bf16[1536,256]{1,0:T(8,128)(2,1)S(1)} %rounded.1), channel_id=1, source_target_pairs={{0,1},{2,3},{4,5},{6,7},{8,9},{10,11},{12,13},{14,15},{16,17},{18,... | collective-permute-start | bytes 2359304 | tf_op jit(solution)/shard_map/ppermute | solution.py:331
  4.9 23.2 %collective-permute-start.4 = (bf16[1536,256]{1,0:T(8,128)(2,1)S(1)}, bf16[1536,256]{1,0:T(8,128)(2,1)}, u32[]{:S(2)}, u32[]{:S(2)}) collective-permute-start(bf16[1536,256]{1,0:T(8,128)(2,1)S(1)} %rounded.1), channel_id=1, source_target_pairs={{0,2},{1,3},{2,4},{3,5},{4,6},{5,7},{6,8},{7,9},{8,10},{9,11},{10,... | collective-permute-start | bytes 2359304 | tf_op jit(solution)/shard_map/ppermute | solution.py:298
  7.8 5.1 %collective-permute-start = (f32[8,128]{1,0:T(8,128)S(1)}, f32[8,128]{1,0:T(8,128)S(1)}, u32[]{:S(2)}, u32[]{:S(2)}) collective-permute-start(f32[8,128]{1,0:T(8,128)S(1)} %bitcast_reduce_fusion), channel_id=1, source_target_pairs={{0,16},{16,0},{32,48},{48,32},{64,80},{80,64},{96,112},{112,96},{1... | collective-permute-start | bytes 12296 | tf_op jit(solution)/shard_map/ppermute | solution.py:318
  12.9 6.4 %collective-permute-start.2 = (f32[8,128]{1,0:T(8,128)S(1)}, f32[8,128]{1,0:T(8,128)S(1)}, u32[]{:S(2)}, u32[]{:S(2)}) collective-permute-start(f32[8,128]{1,0:T(8,128)S(1)} %add.49), channel_id=1, source_target_pairs={{0,32},{16,48},{32,0},{48,16},{64,96},{80,112},{96,64},{112,80},{1... | collective-permute-start | bytes 12296 | tf_op jit(solution)/shard_map/ppermute | solution.py:318
  14.6 7.9 %copy-start.1 = (f32[768,256]{1,0:T(8,128)S(1)}, f32[768,256]{1,0:T(8,128)}, u32[]{:S(2)}) copy-start(f32[768,256]{1,0:T(8,128)} %row_emb.4) | copy-start | bytes 2359300
  14.6 7.9 %copy-start.4 = (f32[768,256]{1,0:T(8,128)S(1)}, f32[768,256]{1,0:T(8,128)}, u32[]{:S(2)}) copy-start(f32[768,256]{1,0:T(8,128)} %col_emb.4) | copy-start | bytes 2359300
  19.4 4.1 %collective-permute-start.3 = (f32[8,128]{1,0:T(8,128)S(1)}, f32[8,128]{1,0:T(8,128)S(1)}, u32[]{:S(2)}, u32[]{:S(2)}) collective-permute-start(f32[8,128]{1,0:T(8,128)S(1)} %add.50), channel_id=1, source_target_pairs={{0,64},{16,80},{32,96},{48,112},{64,0},{80,16},{96,32},{112,48},{1... | collective-permute-start | bytes 12296 | tf_op jit(solution)/shard_map/ppermute | solution.py:318
  22.9 0.6 copy-start.10
  22.9 0.6 copy-start.12
  23.5 5.5 %collective-permute-start.5 = (f32[8,128]{1,0:T(8,128)S(1)}, f32[8,128]{1,0:T(8,128)S(1)}, u32[]{:S(2)}, u32[]{:S(2)}) collective-permute-start(f32[8,128]{1,0:T(8,128)S(1)} %add.61.total), channel_id=1, source_target_pairs={{0,192},{16,208},{32,224},{48,240},{64,128},{80,144},{96,160},{112... | collective-permute-start | bytes 12296 | tf_op jit(solution)/shard_map/ppermute | solution.py:318
  29.0 14.0 %collective-permute-start.9 = (bf16[1536,256]{1,0:T(8,128)(2,1)}, bf16[1536,256]{1,0:T(8,128)(2,1)}, u32[]{:S(2)}, u32[]{:S(2)}) collective-permute-start(bf16[1536,256]{1,0:T(8,128)(2,1)} %collective-permute-done.4.refs_0_), channel_id=1, source_target_pairs={{0,1},{1,0},{2,3},{3,2},{4,5},{5,4},{6,7},{7,6},{8,9},{9,8},{10,11... | collective-permute-start | bytes 2359304 | tf_op jit(solution)/shard_map/ppermute | solution.py:298
  33.1 19.4 %collective-permute-start.6 = (bf16[1536,256]{1,0:T(8,128)(2,1)}, bf16[1536,256]{1,0:T(8,128)(2,1)S(1)}, u32[]{:S(2)}, u32[]{:S(2)}) collective-permute-start(bf16[1536,256]{1,0:T(8,128)(2,1)} %collective-permute-done.4.refs_0_), channel_id=1, source_target_pairs={{0,2},{1,3},{2,4},{3,5},{4,6},{5,7},{6,8},{7,9},{8,10},{9,11},{10,... | collective-permute-start | bytes 2359304 | tf_op jit(solution)/shard_map/ppermute | solution.py:298
  34.9 1.7 %copy-start.8 = (s32[768,768]{1,0:T(8,128)S(1)}, s32[768,768]{1,0:T(8,128)}, u32[]{:S(2)}) copy-start(s32[768,768]{1,0:T(8,128)} %get-tuple-element.96.laid) | copy-start | bytes 7077892
  36.6 0.7 copy-start.13
  37.2 5.8 %copy-start.6 = (s32[768,768]{1,0:T(8,128)S(1)}, s32[768,768]{1,0:T(8,128)}, u32[]{:S(2)}) copy-start(s32[768,768]{1,0:T(8,128)} %get-tuple-element.94.laid) | copy-start | bytes 7077892
  37.2 5.8 %copy-start.11 = (f32[1,768]{1,0:T(1,128)S(1)}, f32[1,768]{1,0:T(1,128)}, u32[]{:S(2)}) copy-start(f32[1,768]{1,0:T(1,128)} %copy-done.10) | copy-start | bytes 9220
  42.4 5.8 %collective-permute-start.10 = (bf16[256,768]{1,0:T(8,128)(2,1)S(1)}, bf16[256,768]{1,0:T(8,128)(2,1)S(1)}, u32[]{:S(2)}, u32[]{:S(2)}) collective-permute-start(bf16[256,768]{1,0:T(8,128)(2,1)S(1)} %get-tuple-element.102), channel_id=1, source_target_pairs={{0,1},{1,0},{2,3},{3,2},{4,5},{5,4},{6,7},{7,6},{8,9},{9,8},{10,11... | collective-permute-start | bytes 1179656 | tf_op jit(solution)/shard_map/ppermute | solution.py:298
  42.8 5.5 %collective-permute-start.11 = (bf16[256,768]{1,0:T(8,128)(2,1)S(1)}, bf16[256,768]{1,0:T(8,128)(2,1)S(1)}, u32[]{:S(2)}, u32[]{:S(2)}) collective-permute-start(bf16[256,768]{1,0:T(8,128)(2,1)S(1)} %get-tuple-element.103), channel_id=1, source_target_pairs={{0,1},{1,0},{2,3},{3,2},{4,5},{5,4},{6,7},{7,6},{8,9},{9,8},{10,11... | collective-permute-start | bytes 1179656 | tf_op jit(solution)/shard_map/ppermute | solution.py:298
  48.2 8.3 %copy-start.7 = (s32[768,768]{1,0:T(8,128)S(1)}, s32[768,768]{1,0:T(8,128)}, u32[]{:S(2)}) copy-start(s32[768,768]{1,0:T(8,128)} %get-tuple-element.92.laid) | copy-start | bytes 7077892
  48.3 23.1 %collective-permute-start.14 = (bf16[512,768]{1,0:T(8,128)(2,1)S(1)}, bf16[512,768]{1,0:T(8,128)(2,1)S(1)}, u32[]{:S(2)}, u32[]{:S(2)}) collective-permute-start(bf16[512,768]{1,0:T(8,128)(2,1)S(1)} %join.2), channel_id=1, source_target_pairs={{0,15},{1,14},{2,1},{3,0},{4,3},{5,2},{6,5},{7,4},{8,7},{9,6},{10,... | collective-permute-start | bytes 2359304 | tf_op jit(solution)/shard_map/ppermute | solution.py:298
  52.5 8.7 %collective-permute-start.7 = (bf16[768,256]{1,0:T(8,128)(2,1)S(1)}, bf16[768,256]{1,0:T(8,128)(2,1)S(1)}, u32[]{:S(2)}, u32[]{:S(2)}) collective-permute-start(bf16[768,256]{1,0:T(8,128)(2,1)S(1)} %get-tuple-element.117), channel_id=1, source_target_pairs={{1,0},{3,2},{5,4},{7,6},{9,8},{11,10},{13,12},{15,14},{17,16},{19,... | collective-permute-start | bytes 1179656 | tf_op jit(solution)/shard_map/ppermute | solution.py:371
  55.2 6.0 %collective-permute-start.8 = (bf16[768,256]{1,0:T(8,128)(2,1)S(1)}, bf16[768,256]{1,0:T(8,128)(2,1)S(1)}, u32[]{:S(2)}, u32[]{:S(2)}) collective-permute-start(bf16[768,256]{1,0:T(8,128)(2,1)S(1)} %get-tuple-element.116), channel_id=1, source_target_pairs={{1,0},{3,2},{5,4},{7,6},{9,8},{11,10},{13,12},{15,14},{17,16},{19,... | collective-permute-start | bytes 1179656 | tf_op jit(solution)/shard_map/ppermute | solution.py:371
  56.6 4.7 %copy-start.15 = (f32[768]{0:T(1024)S(1)}, f32[768]{0:T(1024)}, u32[]{:S(2)}) copy-start(f32[768]{0:T(1024)} %param.8) | copy-start | bytes 9220
  56.6 4.7 %copy-start.16 = (f32[768]{0:T(1024)S(1)}, f32[768]{0:T(1024)}, u32[]{:S(2)}) copy-start(f32[768]{0:T(1024)} %param.9) | copy-start | bytes 9220
  56.6 4.7 %copy-start.9 = (s32[768,768]{1,0:T(8,128)S(1)}, s32[768,768]{1,0:T(8,128)}, u32[]{:S(2)}) copy-start(s32[768,768]{1,0:T(8,128)} %get-tuple-element.70.laid) | copy-start | bytes 7077892
  60.6 5.3 %collective-permute-start.12 = (bf16[256,768]{1,0:T(8,128)(2,1)S(1)}, bf16[256,768]{1,0:T(8,128)(2,1)S(1)}, u32[]{:S(2)}, u32[]{:S(2)}) collective-permute-start(bf16[256,768]{1,0:T(8,128)(2,1)S(1)} %get-tuple-element.109), channel_id=1, source_target_pairs={{0,1},{1,0},{2,3},{3,2},{4,5},{5,4},{6,7},{7,6},{8,9},{9,8},{10,11... | collective-permute-start | bytes 1179656 | tf_op jit(solution)/shard_map/ppermute | solution.py:298
  60.7 5.2 %collective-permute-start.13 = (bf16[256,768]{1,0:T(8,128)(2,1)S(1)}, bf16[256,768]{1,0:T(8,128)(2,1)S(1)}, u32[]{:S(2)}, u32[]{:S(2)}) collective-permute-start(bf16[256,768]{1,0:T(8,128)(2,1)S(1)} %get-tuple-element.110), channel_id=1, source_target_pairs={{0,1},{1,0},{2,3},{3,2},{4,5},{5,4},{6,7},{7,6},{8,9},{9,8},{10,11... | collective-permute-start | bytes 1179656 | tf_op jit(solution)/shard_map/ppermute | solution.py:298
  65.3 6.6 %collective-permute-start.16 = (bf16[256,768]{1,0:T(8,128)(2,1)S(1)}, bf16[256,768]{1,0:T(8,128)(2,1)S(1)}, u32[]{:S(2)}, u32[]{:S(2)}) collective-permute-start(bf16[256,768]{1,0:T(8,128)(2,1)S(1)} %get-tuple-element.107.row_here), channel_id=1, source_target_pairs={{0,1},{1,0},{2,3},{3,2},{4,5},{5,4},{6,7},{7,6},{8,9},{9,8},{10,11... | collective-permute-start | bytes 1179656 | tf_op jit(solution)/shard_map/ppermute | solution.py:298
  65.7 6.2 %collective-permute-start.17 = (bf16[256,768]{1,0:T(8,128)(2,1)S(1)}, bf16[256,768]{1,0:T(8,128)(2,1)S(1)}, u32[]{:S(2)}, u32[]{:S(2)}) collective-permute-start(bf16[256,768]{1,0:T(8,128)(2,1)S(1)} %get-tuple-element.108.col_here), channel_id=1, source_target_pairs={{0,1},{1,0},{2,3},{3,2},{4,5},{5,4},{6,7},{7,6},{8,9},{9,8},{10,11... | collective-permute-start | bytes 1179656 | tf_op jit(solution)/shard_map/ppermute | solution.py:298
  66.0 23.5 %collective-permute-start.15 = (bf16[512,768]{1,0:T(8,128)(2,1)S(1)}, bf16[512,768]{1,0:T(8,128)(2,1)S(1)}, u32[]{:S(2)}, u32[]{:S(2)}) collective-permute-start(bf16[512,768]{1,0:T(8,128)(2,1)S(1)} %join.3), channel_id=1, source_target_pairs={{0,13},{1,12},{2,15},{3,14},{4,1},{5,0},{6,3},{7,2},{8,5},{9,4},{1... | collective-permute-start | bytes 2359304 | tf_op jit(solution)/shard_map/ppermute | solution.py:298
  66.7 22.8 %copy-start.2 = (f32[768,256]{1,0:T(8,128)S(1)}, f32[768,256]{1,0:T(8,128)}, u32[]{:S(2)}) copy-start(f32[768,256]{1,0:T(8,128)} %row_emb.4) | copy-start | bytes 2359300
  66.7 22.8 %copy-start.5 = (f32[768,256]{1,0:T(8,128)S(1)}, f32[768,256]{1,0:T(8,128)}, u32[]{:S(2)}) copy-start(f32[768,256]{1,0:T(8,128)} %col_emb.4) | copy-start | bytes 2359300

commit v2 on v1

--- a/solution.py
+++ b/solution.py
@@ -112,21 +112,16 @@
 ):
     block = own_half.shape[0] // 2
     width = own_half.shape[1]
-    parts = refs[: {"whole": 1, "halves": 2, "either": 3}[kind]]
+    parts = refs[: {"whole": 1, "either": 2}[kind]]
     refs = refs[len(parts) :]
     acc_in, (acc, back_row, back_col, tiles, sems) = (None, refs) if first else (refs[0], refs[1:])
     even = even_ref[0] == 1
 
     def partner(side, j):
+        at = pl.ds(side * block + start + j * cols, cols)
         if kind == "whole":
-            return parts[0][pl.ds(side * block + start + j * cols, cols), :]
-        if kind == "halves":
-            return parts[side][pl.ds(start + j * cols, cols), :]
-        return jnp.where(
-            even,
-            parts[side][pl.ds(start + j * cols, cols), :],
-            parts[2][pl.ds(side * block + start + j * cols, cols), :],
-        )
+            return parts[0][at, :]
+        return jnp.where(even, parts[0][at, :], parts[1][at, :])
 
     copies = [
         pltpu.make_async_copy(
@@ -173,7 +168,7 @@
 def tile(even, laid, totals, lm_rows, lm_cols, own_half, own_t, parts, acc, start, span, rows=768, cols=256):
     block, width = own_half.shape[0] // 2, own_half.shape[1]
     cols = min(cols, span)
-    kind = ("whole", "halves", "either")[len(parts) - 1]
+    kind = ("whole", "either")[len(parts) - 1]
     first = acc is None
     return pl.pallas_call(
         functools.partial(tile_kernel, start=start, span=span, rows=rows, cols=cols, kind=kind, first=first),
@@ -368,11 +363,11 @@
     near_out = [moved(joined, -1, -3)]
     acc, joined = lax.optimization_barrier((acc, joined))
     chip_out, far_out = [], []
-    other = [lax.ppermute(far_in[i * block : (i + 1) * block], "blk", to_even) for i in range(2)]
+    other = lax.ppermute(far_in, "blk", to_even)
     for start, span in zip(starts_of(FAR), FAR):
         acc, back_four = tiles(2, [far_in], acc, start, span)
         from_other = both(swapped, back_four)
-        acc, back_far = tiles(3, [*other, beside], acc, start, span)
+        acc, back_far = tiles(3, [other, beside], acc, start, span)
         joined = join(even, back_far, from_other)
         far_out.append(moved(joined, -3, -5))
         acc, joined = lax.optimization_barrier((acc, joined))

time: 93.2 us -> 100 us (1.073); the launches traced: 91.5 us -> 99.7 us
  starting transfers between devices: 26.5 us -> 32.2 us
  local copies, waits for them, and re-layouts: 4.8 us -> 6.19 us
  waiting for transfers between devices: 27.8 us -> 29 us
    ppermute x11, starting transfers between devices: 11.4 us -> 14.4 us  [moved(): return lax.ppermute(array, 'blk', route)]
    ppermute x2 -> x1, starting transfers between devices: 4.03 us -> 6.67 us  [per_device(): other = lax.ppermute(far_in, 'blk', to_even)]
    unnamed x34, local copies, waits for them, and re-layouts: 4.71 us -> 6.14 us
    ppermute x11, waiting for transfers between devices: 26.3 us -> 27.5 us  [moved(): return lax.ppermute(array, 'blk', route)]
  transfers between devices with their start and end apart: 18 -> 17, of which waited for: 5 -> 5; matrix products, arithmetic and copies ran while one was open for 0% -> 0% of each run, Pallas kernels for 31% -> 29%
where the time goes in v2:
time: 100 us; the launch traced here: 99.7 us
  starting transfers between devices  32.2 us (32%)
  Pallas kernels  30.7 us (31%)
  waiting for transfers between devices  29 us (29%)
  local copies, waits for them, and re-layouts  6.19 us (6%)
    ppermute x11, waiting for transfers between devices, moved(): return lax.ppermute(array, 'blk', route)  27.5 us
    pallas_call x4, Pallas kernels, tile(): pl.pallas_call(functools.partial(tile_kernel, start=start, span=span, row...  18.3 us
    ppermute x11, starting transfers between devices, moved(): return lax.ppermute(array, 'blk', route)  14.4 us
    ppermute x4, starting transfers between devices, from_reach(): return lax.ppermute(total, 'slab', [(i, i ^ reach) for i in range(slabs)])  9.82 us
    pallas_call x2, Pallas kernels, lay(): pl.pallas_call(functools.partial(lay_kernel, base=base), in_specs=[SMEM,...  9.29 us
    ppermute x1, starting transfers between devices, per_device(): other = lax.ppermute(far_in, 'blk', to_even)  6.67 us
    unnamed x34, local copies, waits for them, and re-layouts  6.14 us
    pallas_call x1, Pallas kernels, update(): pl.pallas_call(update_kernel, in_specs=[SMEM] + [VMEM] * (5 + 3 * len(far...  2.05 us
  transfers between devices with their start and end apart: 17, of which 5 were waited for; matrix products, arithmetic and copies ran while one was open for 0% of the time, Pallas kernels for 29%

profile of v2, /device:TPU:7, one launch (start us, length us, event | category | flops | bytes accessed | tf_op | source)
XLA Modules:
  0.0 99.7 jit_solution(10800131678380539412)
XLA Ops:
  0.6 0.0 copy-start
  0.7 1.1 %copy-done = f32[768,256]{1,0:T(8,128)S(1)} copy-done((f32[768,256]{1,0:T(8,128)S(1)}, f32[768,256]{1,0:T(8,128)}, u32[]{:S(2)}) %copy-start) | copy-done | bytes 786456
  1.8 1.1 %copy-done.3 = f32[768,256]{1,0:T(8,128)S(1)} copy-done((f32[768,256]{1,0:T(8,128)S(1)}, f32[768,256]{1,0:T(8,128)}, u32[]{:S(2)}) %copy-start.3) | copy-done | bytes 786456
  2.9 0.1 rounded.1
  3.0 0.6 pad_add_fusion.k_ref
  3.6 1.3 %collective-permute-start.1 = (bf16[1536,256]{1,0:T(8,128)(2,1)S(1)}, bf16[1536,256]{1,0:T(8,128)(2,1)S(1)}, u32[]{:S(2)}, u32[]{:S(2)}) collective-permute-start(bf16[1536,256]{1,0:T(8,128)(2,1)S(1)} %rounded.1), channel_id=1, source_target_pairs={{0,1},{2,3},{4,5},{6,7},{8,9},{10,11},{12,13},{14,15},{16,17},{18,... | collective-permute-start | bytes 2359304 | tf_op jit(solution)/shard_map/ppermute | solution.py:326
  4.9 2.9 %collective-permute-start.4 = (bf16[1536,256]{1,0:T(8,128)(2,1)S(1)}, bf16[1536,256]{1,0:T(8,128)(2,1)}, u32[]{:S(2)}, u32[]{:S(2)}) collective-permute-start(bf16[1536,256]{1,0:T(8,128)(2,1)S(1)} %rounded.1), channel_id=1, source_target_pairs={{0,2},{1,3},{2,4},{3,5},{4,6},{5,7},{6,8},{7,9},{8,10},{9,11},{10,... | collective-permute-start | bytes 2359304 | tf_op jit(solution)/shard_map/ppermute | solution.py:293
  7.8 0.0 copy-done.14
  7.8 0.5 collective-permute-start
  8.3 4.6 %lay.2 = (s32[768,768]{1,0:T(8,128)}, s32[768,768]{1,0:T(8,128)}) custom-call(s32[4]{0:T(128)} %pad_add_fusion.k_ref, s32[768,4,768]{2,1,0:T(4,128)} %counts.3), custom_call_target="tpu_custom_call" | custom-call | flops 1048576 | bytes 1024 | tf_op jit(solution)/shard_map/lay/pallas_call | solution.py:93
  12.9 0.0 collective-permute-done
  12.9 1.7 %collective-permute-start.2 = (f32[8,128]{1,0:T(8,128)S(1)}, f32[8,128]{1,0:T(8,128)S(1)}, u32[]{:S(2)}, u32[]{:S(2)}) collective-permute-start(f32[8,128]{1,0:T(8,128)S(1)} %add.49), channel_id=1, source_target_pairs={{0,32},{16,48},{32,0},{48,16},{64,96},{80,112},{96,64},{112,80},{1... | collective-permute-start | bytes 12296 | tf_op jit(solution)/shard_map/ppermute | solution.py:313
  14.7 4.7 %lay.3 = (s32[768,768]{1,0:T(8,128)}, s32[768,768]{1,0:T(8,128)}) custom-call(s32[4]{0:T(128)} %pad_add_fusion.k_ref, s32[768,4,768]{2,1,0:T(4,128)} %counts.3), custom_call_target="tpu_custom_call" | custom-call | flops 1048576 | bytes 1024 | tf_op jit(solution)/shard_map/lay/pallas_call | solution.py:93
  19.4 0.0 collective-permute-done.2
  19.4 0.0 collective-permute-done.1.refs_1_
  19.4 3.1 %collective-permute-start.3 = (f32[8,128]{1,0:T(8,128)S(1)}, f32[8,128]{1,0:T(8,128)S(1)}, u32[]{:S(2)}, u32[]{:S(2)}) collective-permute-start(f32[8,128]{1,0:T(8,128)S(1)} %add.50), channel_id=1, source_target_pairs={{0,64},{16,80},{32,96},{48,112},{64,0},{80,16},{96,32},{112,48},{1... | collective-permute-start | bytes 12296 | tf_op jit(solution)/shard_map/ppermute | solution.py:313
  22.5 0.0 copy-done.1
  22.5 0.0 copy-done.4
  22.5 0.4 turned.1
  22.9 0.0 copy-start.10
  22.9 0.0 copy-start.12
  22.9 0.5 collective-permute-done.3
  23.5 0.0 copy-done.10
  23.5 0.0 copy-done.12
  23.5 4.5 %collective-permute-start.5 = (f32[8,128]{1,0:T(8,128)S(1)}, f32[8,128]{1,0:T(8,128)S(1)}, u32[]{:S(2)}, u32[]{:S(2)}) collective-permute-start(f32[8,128]{1,0:T(8,128)S(1)} %add.61.total), channel_id=1, source_target_pairs={{0,192},{16,208},{32,224},{48,240},{64,128},{80,144},{96,160},{112... | collective-permute-start | bytes 12296 | tf_op jit(solution)/shard_map/ppermute | solution.py:313
  28.1 0.0 collective-permute-done.4.refs_0_
  28.1 1.0 collective-permute-done.5.more_total
  29.1 2.2 %collective-permute-start.6 = (bf16[1536,256]{1,0:T(8,128)(2,1)}, bf16[1536,256]{1,0:T(8,128)(2,1)S(1)}, u32[]{:S(2)}, u32[]{:S(2)}) collective-permute-start(bf16[1536,256]{1,0:T(8,128)(2,1)} %collective-permute-done.4.refs_0_), channel_id=1, source_target_pairs={{0,2},{1,3},{2,4},{3,5},{4,6},{5,7},{6,8},{7,9},{8,10},{9,11},{10,... | collective-permute-start | bytes 2359304 | tf_op jit(solution)/shard_map/ppermute | solution.py:293
  31.3 3.9 %collective-permute-start.8 = (bf16[1536,256]{1,0:T(8,128)(2,1)}, bf16[1536,256]{1,0:T(8,128)(2,1)}, u32[]{:S(2)}, u32[]{:S(2)}) collective-permute-start(bf16[1536,256]{1,0:T(8,128)(2,1)} %collective-permute-done.4.refs_0_), channel_id=1, source_target_pairs={{0,1},{1,0},{2,3},{3,2},{4,5},{5,4},{6,7},{7,6},{8,9},{9,8},{10,11... | collective-permute-start | bytes 2359304 | tf_op jit(solution)/shard_map/ppermute | solution.py:293
  35.2 1.7 %copy-done.8 = s32[768,768]{1,0:T(8,128)S(1)} copy-done((s32[768,768]{1,0:T(8,128)S(1)}, s32[768,768]{1,0:T(8,128)}, u32[]{:S(2)}) %copy-start.8) | copy-done | bytes 2359320
  36.8 0.7 copy-done.13
  37.5 5.2 %tile.4 = (f32[1536,256]{1,0:T(8,128)S(1)}, bf16[256,768]{1,0:T(8,128)(2,1)S(1)}, bf16[256,768]{1,0:T(8,128)(2,1)S(1)}) custom-call(s32[1]{0:T(128)} %bitcast.even_ref, s32[768,768]{1,0:T(8,128)S(1)} %copy-done.8, f32[8,128]{1,0:T(8,128)S(1)} %add.61.total, f32[8,128]{1,0:T(8,128)S(1)} %collective-permute-done.5.more_total, ...), custom_call_target="tpu_custom_call" | custom-call | flops 1048576 | bytes 1024 | tf_op jit(solution)/shard_map/tile/pallas_call | solution.py:173
  42.7 0.1 collective-permute-start.10
  42.8 0.5 collective-permute-start.9
  43.3 1.5 %collective-permute-done.6.refs_0_ = bf16[1536,256]{1,0:T(8,128)(2,1)S(1)} collective-permute-done((bf16[1536,256]{1,0:T(8,128)(2,1)}, bf16[1536,256]{1,0:T(8,128)(2,1)S(1)}, u32[]{:S(2)}, u32[]{:S(2)}) %collective-permute-start.6) | collective-permute-done | bytes 786464 | tf_op jit(solution)/shard_map/ppermute | solution.py:293
  44.8 6.7 %collective-permute-start.7 = (bf16[1536,256]{1,0:T(8,128)(2,1)S(1)}, bf16[1536,256]{1,0:T(8,128)(2,1)S(1)}, u32[]{:S(2)}, u32[]{:S(2)}) collective-permute-start(bf16[1536,256]{1,0:T(8,128)(2,1)S(1)} %collective-permute-done.6.refs_0_), channel_id=1, source_target_pairs={{1,0},{3,2},{5,4},{7,6},{9,8},{11,10},{13,12},{15,14},{17,16},{19,... | collective-permute-start | bytes 2359304 | tf_op jit(solution)/shard_map/ppermute | solution.py:366
  51.5 0.0 collective-permute-done.8.refs_0_
  51.5 0.0 copy-done.6
  51.5 0.0 copy-done.11
  51.5 5.1 %tile.5 = (f32[1536,256]{1,0:T(8,128)S(1)}, bf16[256,768]{1,0:T(8,128)(2,1)S(1)}, bf16[256,768]{1,0:T(8,128)(2,1)S(1)}) custom-call(s32[1]{0:T(128)} %bitcast.even_ref, s32[768,768]{1,0:T(8,128)S(1)} %copy-done.6, f32[8,128]{1,0:T(8,128)S(1)} %add.61.total, f32[8,128]{1,0:T(8,128)S(1)} %collective-permute-done.5.more_total, ...), custom_call_target="tpu_custom_call", output_to_operand_aliasing={{0}: (9, {})} | custom-call | flops 1048576 | bytes 1024 | tf_op jit(solution)/shard_map/tile/pallas_call | solution.py:173
  56.6 0.0 copy-start.7
  56.7 0.0 collective-permute-done.10.col_there
  56.7 0.0 collective-permute-done.9.row_there
  56.7 0.1 join.2
  56.8 0.1 collective-permute-start.13
  56.9 1.4 %copy-done.7 = s32[768,768]{1,0:T(8,128)S(1)} copy-done((s32[768,768]{1,0:T(8,128)S(1)}, s32[768,768]{1,0:T(8,128)}, u32[]{:S(2)}) %copy-start.7) | copy-done | bytes 2359320
  58.3 4.0 %tile.6 = (f32[1536,256]{1,0:T(8,128)S(1)}, bf16[256,768]{1,0:T(8,128)(2,1)S(1)}, bf16[256,768]{1,0:T(8,128)(2,1)S(1)}) custom-call(s32[1]{0:T(128)} %bitcast.even_ref, s32[768,768]{1,0:T(8,128)S(1)} %copy-done.7, f32[8,128]{1,0:T(8,128)S(1)} %add.61.total, f32[8,128]{1,0:T(8,128)S(1)} %collective-permute-done.5.more_total, ...), custom_call_target="tpu_custom_call", output_to_operand_aliasing={{0}: (9, {})} | custom-call | flops 1048576 | bytes 1024 | tf_op jit(solution)/shard_map/tile/pallas_call | solution.py:173
  62.3 0.1 collective-permute-start.11
  62.4 0.5 collective-permute-start.12
  63.0 0.0 collective-permute-done.7.refs_0_
  63.0 0.0 copy-done.9
  63.0 4.0 %tile.7 = (f32[1536,256]{1,0:T(8,128)S(1)}, bf16[256,768]{1,0:T(8,128)(2,1)S(1)}, bf16[256,768]{1,0:T(8,128)(2,1)S(1)}) custom-call(s32[1]{0:T(128)} %bitcast.even_ref, s32[768,768]{1,0:T(8,128)S(1)} %copy-done.9, f32[8,128]{1,0:T(8,128)S(1)} %add.61.total, f32[8,128]{1,0:T(8,128)S(1)} %collective-permute-done.5.more_total, ...), custom_call_target="tpu_custom_call", output_to_operand_aliasing={{0}: (10, {})} | custom-call | flops 1048576 | bytes 1024 | tf_op jit(solution)/shard_map/tile/pallas_call | solution.py:173
  67.0 0.4 collective-permute-start.15
  67.4 0.2 collective-permute-start.16
  67.6 0.0 collective-permute-done.11.row_there
  67.6 0.0 collective-permute-done.12.col_there
  67.6 0.1 join.3
  67.7 3.5 %collective-permute-start.14 = (bf16[512,768]{1,0:T(8,128)(2,1)S(1)}, bf16[512,768]{1,0:T(8,128)(2,1)S(1)}, u32[]{:S(2)}, u32[]{:S(2)}) collective-permute-start(bf16[512,768]{1,0:T(8,128)(2,1)S(1)} %join.3), channel_id=1, source_target_pairs={{0,13},{1,12},{2,15},{3,14},{4,1},{5,0},{6,3},{7,2},{8,5},{9,4},{1... | collective-permute-start | bytes 2359304 | tf_op jit(solution)/shard_map/ppermute | solution.py:293
  71.2 10.2 %collective-permute-done.13.refs_0_ = bf16[512,768]{1,0:T(8,128)(2,1)S(1)} collective-permute-done((bf16[512,768]{1,0:T(8,128)(2,1)S(1)}, bf16[512,768]{1,0:T(8,128)(2,1)S(1)}, u32[]{:S(2)}, u32[]{:S(2)}) %collective-permute-start.13) | collective-permute-done | bytes 786464 | tf_op jit(solution)/shard_map/ppermute | solution.py:293
  81.4 0.5 gather_up.1.grads
  81.9 0.0 collective-permute-done.15.refs_1_
  81.9 0.0 collective-permute-done.16.refs_2_
  81.9 15.7 %collective-permute-done.14.refs_0_ = bf16[512,768]{1,0:T(8,128)(2,1)S(1)} collective-permute-done((bf16[512,768]{1,0:T(8,128)(2,1)S(1)}, bf16[512,768]{1,0:T(8,128)(2,1)S(1)}, u32[]{:S(2)}, u32[]{:S(2)}) %collective-permute-start.14) | collective-permute-done | bytes 786464 | tf_op jit(solution)/shard_map/ppermute | solution.py:293
  97.6 2.0 %update.1 = (f32[768,256]{1,0:T(8,128)}, f32[768,256]{1,0:T(8,128)}, f32[6,128]{1,0:T(8,128)}, f32[6,128]{1,0:T(8,128)}) custom-call(s32[1]{0:T(128)} %bitcast.even_ref, f32[768,256]{1,0:T(8,128)S(1)} %copy-done.2, f32[768,256]{1,0:T(8,128)S(1)} %copy-done.5, f32[1,768]{1,0:T(1,128)S(1)} %reshape.30.row_acc, f32[1,768]{1,0:T(1,128)S(1)} %reshape.31.col_acc, ...), custom_call_target="tpu_custom_call" | custom-call | flops 1048576 | bytes 1024 | tf_op jit(solution)/shard_map/update/pallas_call | solution.py:271
  (26 shorter events, 0.1 us)
Async XLA Ops:
  0.6 1.1 %copy-start = (f32[768,256]{1,0:T(8,128)S(1)}, f32[768,256]{1,0:T(8,128)}, u32[]{:S(2)}) copy-start(f32[768,256]{1,0:T(8,128)} %row_emb.4) | copy-start | bytes 2359300
  1.8 1.1 %copy-start.3 = (f32[768,256]{1,0:T(8,128)S(1)}, f32[768,256]{1,0:T(8,128)}, u32[]{:S(2)}) copy-start(f32[768,256]{1,0:T(8,128)} %col_emb.4) | copy-start | bytes 2359300
  2.9 4.9 %copy-start.14 = (s32[12288]{0:T(1024)S(1)}, s32[12288]{0:T(1024)}, u32[]{:S(2)}) copy-start(s32[12288]{0:T(1024)} %param.11) | copy-start | bytes 147460
  3.6 15.8 %collective-permute-start.1 = (bf16[1536,256]{1,0:T(8,128)(2,1)S(1)}, bf16[1536,256]{1,0:T(8,128)(2,1)S(1)}, u32[]{:S(2)}, u32[]{:S(2)}) collective-permute-start(bf16[1536,256]{1,0:T(8,128)(2,1)S(1)} %rounded.1), channel_id=1, source_target_pairs={{0,1},{2,3},{4,5},{6,7},{8,9},{10,11},{12,13},{14,15},{16,17},{18,... | collective-permute-start | bytes 2359304 | tf_op jit(solution)/shard_map/ppermute | solution.py:326
  4.9 23.2 %collective-permute-start.4 = (bf16[1536,256]{1,0:T(8,128)(2,1)S(1)}, bf16[1536,256]{1,0:T(8,128)(2,1)}, u32[]{:S(2)}, u32[]{:S(2)}) collective-permute-start(bf16[1536,256]{1,0:T(8,128)(2,1)S(1)} %rounded.1), channel_id=1, source_target_pairs={{0,2},{1,3},{2,4},{3,5},{4,6},{5,7},{6,8},{7,9},{8,10},{9,11},{10,... | collective-permute-start | bytes 2359304 | tf_op jit(solution)/shard_map/ppermute | solution.py:293
  7.8 5.1 %collective-permute-start = (f32[8,128]{1,0:T(8,128)S(1)}, f32[8,128]{1,0:T(8,128)S(1)}, u32[]{:S(2)}, u32[]{:S(2)}) collective-permute-start(f32[8,128]{1,0:T(8,128)S(1)} %bitcast_reduce_fusion), channel_id=1, source_target_pairs={{0,16},{16,0},{32,48},{48,32},{64,80},{80,64},{96,112},{112,96},{1... | collective-permute-start | bytes 12296 | tf_op jit(solution)/shard_map/ppermute | solution.py:313
  12.9 6.4 %collective-permute-start.2 = (f32[8,128]{1,0:T(8,128)S(1)}, f32[8,128]{1,0:T(8,128)S(1)}, u32[]{:S(2)}, u32[]{:S(2)}) collective-permute-start(f32[8,128]{1,0:T(8,128)S(1)} %add.49), channel_id=1, source_target_pairs={{0,32},{16,48},{32,0},{48,16},{64,96},{80,112},{96,64},{112,80},{1... | collective-permute-start | bytes 12296 | tf_op jit(solution)/shard_map/ppermute | solution.py:313
  14.7 7.9 %copy-start.1 = (f32[768,256]{1,0:T(8,128)S(1)}, f32[768,256]{1,0:T(8,128)}, u32[]{:S(2)}) copy-start(f32[768,256]{1,0:T(8,128)} %row_emb.4) | copy-start | bytes 2359300
  14.7 7.9 %copy-start.4 = (f32[768,256]{1,0:T(8,128)S(1)}, f32[768,256]{1,0:T(8,128)}, u32[]{:S(2)}) copy-start(f32[768,256]{1,0:T(8,128)} %col_emb.4) | copy-start | bytes 2359300
  19.4 4.1 %collective-permute-start.3 = (f32[8,128]{1,0:T(8,128)S(1)}, f32[8,128]{1,0:T(8,128)S(1)}, u32[]{:S(2)}, u32[]{:S(2)}) collective-permute-start(f32[8,128]{1,0:T(8,128)S(1)} %add.50), channel_id=1, source_target_pairs={{0,64},{16,80},{32,96},{48,112},{64,0},{80,16},{96,32},{112,48},{1... | collective-permute-start | bytes 12296 | tf_op jit(solution)/shard_map/ppermute | solution.py:313
  22.9 0.6 copy-start.10
  22.9 0.6 copy-start.12
  23.5 5.5 %collective-permute-start.5 = (f32[8,128]{1,0:T(8,128)S(1)}, f32[8,128]{1,0:T(8,128)S(1)}, u32[]{:S(2)}, u32[]{:S(2)}) collective-permute-start(f32[8,128]{1,0:T(8,128)S(1)} %add.61.total), channel_id=1, source_target_pairs={{0,192},{16,208},{32,224},{48,240},{64,128},{80,144},{96,160},{112... | collective-permute-start | bytes 12296 | tf_op jit(solution)/shard_map/ppermute | solution.py:313
  29.1 15.7 %collective-permute-start.6 = (bf16[1536,256]{1,0:T(8,128)(2,1)}, bf16[1536,256]{1,0:T(8,128)(2,1)S(1)}, u32[]{:S(2)}, u32[]{:S(2)}) collective-permute-start(bf16[1536,256]{1,0:T(8,128)(2,1)} %collective-permute-done.4.refs_0_), channel_id=1, source_target_pairs={{0,2},{1,3},{2,4},{3,5},{4,6},{5,7},{6,8},{7,9},{8,10},{9,11},{10,... | collective-permute-start | bytes 2359304 | tf_op jit(solution)/shard_map/ppermute | solution.py:293
  31.3 20.2 %collective-permute-start.8 = (bf16[1536,256]{1,0:T(8,128)(2,1)}, bf16[1536,256]{1,0:T(8,128)(2,1)}, u32[]{:S(2)}, u32[]{:S(2)}) collective-permute-start(bf16[1536,256]{1,0:T(8,128)(2,1)} %collective-permute-done.4.refs_0_), channel_id=1, source_target_pairs={{0,1},{1,0},{2,3},{3,2},{4,5},{5,4},{6,7},{7,6},{8,9},{9,8},{10,11... | collective-permute-start | bytes 2359304 | tf_op jit(solution)/shard_map/ppermute | solution.py:293
  35.2 1.7 %copy-start.8 = (s32[768,768]{1,0:T(8,128)S(1)}, s32[768,768]{1,0:T(8,128)}, u32[]{:S(2)}) copy-start(s32[768,768]{1,0:T(8,128)} %get-tuple-element.96.laid) | copy-start | bytes 7077892
  36.8 0.7 copy-start.13
  37.5 14.0 %copy-start.6 = (s32[768,768]{1,0:T(8,128)S(1)}, s32[768,768]{1,0:T(8,128)}, u32[]{:S(2)}) copy-start(s32[768,768]{1,0:T(8,128)} %get-tuple-element.94.laid) | copy-start | bytes 7077892
  37.5 14.0 %copy-start.11 = (f32[1,768]{1,0:T(1,128)S(1)}, f32[1,768]{1,0:T(1,128)}, u32[]{:S(2)}) copy-start(f32[1,768]{1,0:T(1,128)} %copy-done.10) | copy-start | bytes 9220
  42.7 14.0 %collective-permute-start.10 = (bf16[256,768]{1,0:T(8,128)(2,1)S(1)}, bf16[256,768]{1,0:T(8,128)(2,1)S(1)}, u32[]{:S(2)}, u32[]{:S(2)}) collective-permute-start(bf16[256,768]{1,0:T(8,128)(2,1)S(1)} %get-tuple-element.103), channel_id=1, source_target_pairs={{0,1},{1,0},{2,3},{3,2},{4,5},{5,4},{6,7},{7,6},{8,9},{9,8},{10,11... | collective-permute-start | bytes 1179656 | tf_op jit(solution)/shard_map/ppermute | solution.py:293
  42.8 13.9 %collective-permute-start.9 = (bf16[256,768]{1,0:T(8,128)(2,1)S(1)}, bf16[256,768]{1,0:T(8,128)(2,1)S(1)}, u32[]{:S(2)}, u32[]{:S(2)}) collective-permute-start(bf16[256,768]{1,0:T(8,128)(2,1)S(1)} %get-tuple-element.102), channel_id=1, source_target_pairs={{0,1},{1,0},{2,3},{3,2},{4,5},{5,4},{6,7},{7,6},{8,9},{9,8},{10,11... | collective-permute-start | bytes 1179656 | tf_op jit(solution)/shard_map/ppermute | solution.py:293
  44.8 18.2 %collective-permute-start.7 = (bf16[1536,256]{1,0:T(8,128)(2,1)S(1)}, bf16[1536,256]{1,0:T(8,128)(2,1)S(1)}, u32[]{:S(2)}, u32[]{:S(2)}) collective-permute-start(bf16[1536,256]{1,0:T(8,128)(2,1)S(1)} %collective-permute-done.6.refs_0_), channel_id=1, source_target_pairs={{1,0},{3,2},{5,4},{7,6},{9,8},{11,10},{13,12},{15,14},{17,16},{19,... | collective-permute-start | bytes 2359304 | tf_op jit(solution)/shard_map/ppermute | solution.py:366
  56.6 1.7 %copy-start.7 = (s32[768,768]{1,0:T(8,128)S(1)}, s32[768,768]{1,0:T(8,128)}, u32[]{:S(2)}) copy-start(s32[768,768]{1,0:T(8,128)} %get-tuple-element.92.laid) | copy-start | bytes 7077892
  56.8 24.6 %collective-permute-start.13 = (bf16[512,768]{1,0:T(8,128)(2,1)S(1)}, bf16[512,768]{1,0:T(8,128)(2,1)S(1)}, u32[]{:S(2)}, u32[]{:S(2)}) collective-permute-start(bf16[512,768]{1,0:T(8,128)(2,1)S(1)} %join.2), channel_id=1, source_target_pairs={{0,15},{1,14},{2,1},{3,0},{4,3},{5,2},{6,5},{7,4},{8,7},{9,6},{10,... | collective-permute-start | bytes 2359304 | tf_op jit(solution)/shard_map/ppermute | solution.py:293
  58.3 4.6 %copy-start.15 = (f32[768]{0:T(1024)S(1)}, f32[768]{0:T(1024)}, u32[]{:S(2)}) copy-start(f32[768]{0:T(1024)} %param.8) | copy-start | bytes 9220
  58.3 4.6 %copy-start.16 = (f32[768]{0:T(1024)S(1)}, f32[768]{0:T(1024)}, u32[]{:S(2)}) copy-start(f32[768]{0:T(1024)} %param.9) | copy-start | bytes 9220
  58.3 4.7 %copy-start.9 = (s32[768,768]{1,0:T(8,128)S(1)}, s32[768,768]{1,0:T(8,128)}, u32[]{:S(2)}) copy-start(s32[768,768]{1,0:T(8,128)} %get-tuple-element.70.laid) | copy-start | bytes 7077892
  62.3 5.3 %collective-permute-start.11 = (bf16[256,768]{1,0:T(8,128)(2,1)S(1)}, bf16[256,768]{1,0:T(8,128)(2,1)S(1)}, u32[]{:S(2)}, u32[]{:S(2)}) collective-permute-start(bf16[256,768]{1,0:T(8,128)(2,1)S(1)} %get-tuple-element.109), channel_id=1, source_target_pairs={{0,1},{1,0},{2,3},{3,2},{4,5},{5,4},{6,7},{7,6},{8,9},{9,8},{10,11... | collective-permute-start | bytes 1179656 | tf_op jit(solution)/shard_map/ppermute | solution.py:293
  62.4 5.2 %collective-permute-start.12 = (bf16[256,768]{1,0:T(8,128)(2,1)S(1)}, bf16[256,768]{1,0:T(8,128)(2,1)S(1)}, u32[]{:S(2)}, u32[]{:S(2)}) collective-permute-start(bf16[256,768]{1,0:T(8,128)(2,1)S(1)} %get-tuple-element.110), channel_id=1, source_target_pairs={{0,1},{1,0},{2,3},{3,2},{4,5},{5,4},{6,7},{7,6},{8,9},{9,8},{10,11... | collective-permute-start | bytes 1179656 | tf_op jit(solution)/shard_map/ppermute | solution.py:293
  67.0 14.9 %collective-permute-start.15 = (bf16[256,768]{1,0:T(8,128)(2,1)S(1)}, bf16[256,768]{1,0:T(8,128)(2,1)S(1)}, u32[]{:S(2)}, u32[]{:S(2)}) collective-permute-start(bf16[256,768]{1,0:T(8,128)(2,1)S(1)} %get-tuple-element.107.row_here), channel_id=1, source_target_pairs={{0,1},{1,0},{2,3},{3,2},{4,5},{5,4},{6,7},{7,6},{8,9},{9,8},{10,11... | collective-permute-start | bytes 1179656 | tf_op jit(solution)/shard_map/ppermute | solution.py:293
  67.4 14.5 %collective-permute-start.16 = (bf16[256,768]{1,0:T(8,128)(2,1)S(1)}, bf16[256,768]{1,0:T(8,128)(2,1)S(1)}, u32[]{:S(2)}, u32[]{:S(2)}) collective-permute-start(bf16[256,768]{1,0:T(8,128)(2,1)S(1)} %get-tuple-element.108.col_here), channel_id=1, source_target_pairs={{0,1},{1,0},{2,3},{3,2},{4,5},{5,4},{6,7},{7,6},{8,9},{9,8},{10,11... | collective-permute-start | bytes 1179656 | tf_op jit(solution)/shard_map/ppermute | solution.py:293
  67.7 29.9 %collective-permute-start.14 = (bf16[512,768]{1,0:T(8,128)(2,1)S(1)}, bf16[512,768]{1,0:T(8,128)(2,1)S(1)}, u32[]{:S(2)}, u32[]{:S(2)}) collective-permute-start(bf16[512,768]{1,0:T(8,128)(2,1)S(1)} %join.3), channel_id=1, source_target_pairs={{0,13},{1,12},{2,15},{3,14},{4,1},{5,0},{6,3},{7,2},{8,5},{9,4},{1... | collective-permute-start | bytes 2359304 | tf_op jit(solution)/shard_map/ppermute | solution.py:293
  71.2 26.5 %copy-start.2 = (f32[768,256]{1,0:T(8,128)S(1)}, f32[768,256]{1,0:T(8,128)}, u32[]{:S(2)}) copy-start(f32[768,256]{1,0:T(8,128)} %row_emb.4) | copy-start | bytes 2359300
  71.2 26.5 %copy-start.5 = (f32[768,256]{1,0:T(8,128)S(1)}, f32[768,256]{1,0:T(8,128)}, u32[]{:S(2)}) copy-start(f32[768,256]{1,0:T(8,128)} %col_emb.4) | copy-start | bytes 2359300
